TPU v7x, 128 devices: a whole 4x4x4 slice. The times are simulated.
128 devices in a mesh: box: 8 (over z, core), dir: 16 (over x, y).
Axes of the slice: x: 4, y: 4, z: 4, core: 2. Of those that a mesh axis runs over, the one named last changes fastest.
Arguments:
- currents: bfloat16 [16384, 256, 128], P(('box', 'dir')), may hold values from -6 to 6
- leaf_parent: int32 [16384], P(('box', 'dir')), may hold values from 0 to 255, as said below
- near_links: int32 [16384, 2], P(('box', 'dir')), may hold values 0 or 1
- near_blocks: bfloat16 [3, 256, 256], replicated, may hold values from -0.375 to 0.375
- aggregate_maps: bfloat16 [64, 256, 256], replicated, may hold values from -0.375 to 0.375
- far_boxes: int32 [256, 64], P('box'), may hold values from 0 to 255
- far_counts: int32 [256], P('box'), may hold values from 16 to 64
- translate_coef: float32 [256, 64, 256], P('box'), may hold values from 0.005 to 0.05
- time_kernel: float32 [128], replicated, may hold values from -0.5 to 0.5
- disaggregate_maps: bfloat16 [64, 256, 256], replicated, may hold values from -0.375 to 0.375
Outputs:
- field: bfloat16 [16384, 256, 128], P(('box', 'dir'))
Inputs may be any that keep to these rules, and one draw needn't show every extreme that they name: `leaf_parent`: the leaves k * 64 to (k + 1) * 64 - 1 share one parent. The leaves g * 2048 to (g + 1) * 2048 - 1 have as parents the top-level boxes g * 32 to (g + 1) * 32 - 1, each exactly once as a run.
All inputs are finite; a program needn't handle non-finite values. No bound on the sum of `near_links` on one device may be relied on, other than what follows from the above.
Results may differ from a plain program's by a relative error of at most 0.0047.
Values may be sent and summed in bfloat16 or wider, within the bound.
No kernel may reach another device: no remote copies, remote signals or barrier semaphores. Data moves between devices by JAX's collectives and lax.ppermute only.
A program may use at most 192 MiB of HBM per device.

v0:
```python
import jax
import jax.numpy as jnp
from jax import lax
from jax.sharding import Mesh
from jax.sharding import PartitionSpec as P

LEAF_TOP = 64
BOX = ("box_0", "box_1")
BOX_DIR = ("box_0", "box_1", "dir")


def in_blocks(array, dim, devices):
    before, after = (array.shape[:dim], array.shape[dim + 1 :])
    return jnp.moveaxis(array.reshape(*before, devices, -1, *after), dim, 0)


def summed_on_arrival(array, axis, dim):
    tiles = in_blocks(array, dim, lax.axis_size(axis))
    arrived = lax.all_to_all(tiles, axis, split_axis=0, concat_axis=0, tiled=True)
    return arrived.sum(axis=0)


def edges_of(length, count):
    unit = 8 if length >= 8 * count else 1
    return [length // unit * k // count * unit for k in range(1, count)]


def all_blocks(array, axes, sequence):
    tiles = array[None]
    for k in sequence:
        tiles = lax.all_gather(tiles, axes[k], axis=0, tiled=True)
    held = [lax.axis_size(axes[k]) for k in reversed(sequence)]
    tiles = tiles.reshape(*held, *array.shape)
    turned = sorted(range(len(sequence)), key=lambda place: sequence[len(sequence) - 1 - place])
    return tiles.transpose(*turned, *range(len(sequence), tiles.ndim)).reshape(-1, *array.shape)


def in_order(tiles, dim):
    shape = list(tiles.shape[1:])
    shape[dim] *= tiles.shape[0]
    return jnp.moveaxis(tiles, 0, dim).reshape(shape)


def spread_gather(array, axes, dim):
    numbers = list(range(len(axes)))[::-1]
    cut = array.shape.index(max(array.shape[:-1] or array.shape))
    edges = [0, *edges_of(array.shape[cut], len(axes)), array.shape[cut]]
    done = []
    for k, (start, end) in enumerate(zip(edges, edges[1:])):
        if end > start:
            share = lax.slice_in_dim(array, start, end, axis=cut)
            done.append(all_blocks(share, axes, numbers[k:] + numbers[:k]))
    return in_order(jnp.concatenate(done, axis=cut + 1), dim)


def sent_to_all(array, axis):
    devices = lax.axis_size(axis)
    return lax.all_to_all(
        jnp.broadcast_to(array[None], (devices, *array.shape)), axis, 0, 0, tiled=True
    )


def collect(array, axis, dim):
    return in_order(sent_to_all(array, axis), dim)


def with_halo(block, sides, width):
    for axis, dim in sides:
        count = lax.axis_size(axis)
        forward = [(i, i + 1) for i in range(count - 1)]
        backward = [(target, source) for source, target in forward]
        low = lax.ppermute(
            lax.slice_in_dim(block, block.shape[dim] - width, None, axis=dim), axis, forward
        )
        high = lax.ppermute(lax.slice_in_dim(block, 0, width, axis=dim), axis, backward)
        block = jnp.concatenate([low, block, high], axis=dim)
    return block


def time_matrix(kernel):
    length = kernel.shape[0]
    sample_lag = jnp.arange(length)[:, None] - jnp.arange(length)[None, :]
    return jnp.where(
        sample_lag >= 0, kernel[jnp.clip(sample_lag, 0, length - 1)], jnp.zeros((), kernel.dtype)
    )


def per_device(
    currents,
    leaf_parent,
    near_links,
    near_blocks,
    aggregate_maps,
    far_boxes,
    far_counts,
    translate_coef,
    time_kernel,
    disaggregate_maps,
):
    highest = lax.Precision.HIGHEST
    leaf_count, unknowns, samples = currents.shape
    run_length = min(leaf_count, LEAF_TOP)
    run_count = leaf_count // run_length
    top_local, list_slots = far_boxes.shape
    top_total = top_local * lax.axis_size(BOX)
    direction_total = aggregate_maps.shape[1]
    dir_rows = direction_total // lax.axis_size("dir")
    dir_index = lax.axis_index("dir")
    local_parent = leaf_parent - lax.axis_index(BOX) * top_local
    run_parent = local_parent.reshape(run_count, run_length)[:, 0]
    run_onehot = (run_parent[:, None] == jnp.arange(top_local)[None, :]).astype(jnp.float32)
    leaf_runs = currents.reshape(run_count, run_length, unknowns, samples)
    map_block = aggregate_maps
    run_sums = jnp.einsum("sqp,bspt->bqt", map_block, leaf_runs, preferred_element_type=jnp.float32)
    own_rays = summed_on_arrival(
        jnp.einsum("bc,bqt->qct", run_onehot, run_sums, precision=highest), "dir", 0
    )
    own_rays = own_rays.astype(jnp.bfloat16)
    is_valid = (jnp.arange(list_slots)[None, :] < far_counts[:, None]).astype(jnp.float32)
    matches = (far_boxes[:, :, None] == jnp.arange(top_total)[None, None, :]).astype(
        jnp.float32
    ) * is_valid[:, :, None]
    coef_block = lax.dynamic_slice_in_dim(translate_coef, dir_index * dir_rows, dir_rows, 2)
    weights = jnp.einsum("cfs,cfq->csq", matches, coef_block, precision=highest)
    far_sum = jnp.einsum(
        "csq,qst->cqt",
        weights,
        spread_gather(own_rays, BOX, 1).astype(jnp.float32),
        precision=highest,
    )
    incoming = jnp.einsum(
        "cqs,ts->cqt", far_sum, time_matrix(time_kernel), precision=highest
    ).astype(jnp.bfloat16)
    selected = jnp.einsum(
        "bc,cqt->bqt",
        run_onehot,
        collect(incoming, "dir", 1).astype(jnp.float32),
        precision=highest,
    ).astype(jnp.bfloat16)
    map_block = disaggregate_maps
    far_terms = jnp.einsum("spq,bqt->bspt", map_block, selected, preferred_element_type=jnp.float32)
    far_field = far_terms.reshape(leaf_count, unknowns, samples)
    rim_leaves = jnp.concatenate([currents[:1], currents[-1:]], axis=0)
    extended = with_halo(rim_leaves, ((BOX_DIR, 0),), 1)
    link_mask = near_links.astype(jnp.float32)
    self_term = jnp.einsum(
        "pr,lrt->lpt", near_blocks[0], currents, preferred_element_type=jnp.float32
    )
    before_all = jnp.einsum(
        "pr,lrt->lpt", near_blocks[1], currents, preferred_element_type=jnp.float32
    )
    after_all = jnp.einsum(
        "pr,lrt->lpt", near_blocks[2], currents, preferred_element_type=jnp.float32
    )
    before_rim = jnp.dot(near_blocks[1], extended[0], preferred_element_type=jnp.float32)
    after_rim = jnp.dot(near_blocks[2], extended[3], preferred_element_type=jnp.float32)
    before_term = jnp.concatenate([before_rim[None], before_all[:-1]], axis=0)
    after_term = jnp.concatenate([after_all[1:], after_rim[None]], axis=0)
    near_field = (
        self_term
        + link_mask[:, 0, None, None] * before_term
        + link_mask[:, 1, None, None] * after_term
    )
    return (near_field + far_field).astype(jnp.bfloat16)


def solution(mesh):
    finer = Mesh(mesh.devices.reshape(4, 2, mesh.shape["dir"]), ("box_0", "box_1", "dir"))
    in_specs = (
        P(BOX_DIR, None, None),
        P(BOX_DIR),
        P(BOX_DIR, None),
        P(),
        P(),
        P(BOX, None),
        P(BOX),
        P(BOX, None, None),
        P(),
        P(),
    )
    out_specs = P(BOX_DIR, None, None)
    return jax.shard_map(
        per_device, mesh=finer, in_specs=in_specs, out_specs=out_specs, check_vma=False
    )
```

profile of v0, /device:TPU:1, one launch (start us, length us, event | category | flops | bytes accessed | tf_op | source)
XLA Modules:
  0.0 255.4 jit_solution(14275734861325544151)
XLA Ops:
  0.0 0.0 copy-start
  0.0 0.0 copy-start.7
  0.0 8.3 %fusion.12 = f32[2,256,128]{1,2,0:T(8,128)S(1)} fusion(bf16[2,64,256,128]{3,2,1,0:T(8,128)(2,1)} %bitcast.96, bf16[64,256,256]{2,1,0:T(8,128)(2,1)} %param.14), kind=kOutput, calls=%fused_computation.18 | convolution fusion | flops 2147483648 | bytes 17039360 | tf_op jit(solution)/shard_map/sqp,bspt->bqt/dot_general | solution.py:114
  8.3 0.0 copy-start.4
  8.3 0.0 copy-start.2
  8.3 0.1 copy.60
  8.5 0.0 copy-done.7
  8.5 0.1 reshape.78
  8.6 0.1 slice_reduce_fusion
  8.7 3.9 %fusion.47 = f32[256,128,32]{1,2,0:T(8,128)} fusion(f32[2,256,128]{2,0,1:T(2,128)S(1)} %copy.60, s32[2]{0:T(128)S(1)} %slice_reduce_fusion), kind=kOutput, calls=%fused_computation.56 | convolution fusion | flops 25165888 | bytes 4456456 | tf_op jit(solution)/shard_map/bc,bqt->qct/dot_general | solution.py:116
  12.7 7.6 %all-to-all-start = ((f32[16,16,32,128]{3,2,1,0:T(8,128)}), f32[16,16,32,128]{3,2,1,0:T(8,128)}, u32[]{:S(2)}, u32[]{:S(2)}) async-start(f32[16,16,32,128]{3,2,1,0:T(8,128)} %bitcast.97), calls=%async_computation | async-start | bytes 8388608 | tf_op jit(solution)/shard_map/all_to_all | solution.py:19
  20.3 0.9 fusion.55
  21.2 3.2 %collective-permute-start = (bf16[1,256,128]{2,1,0:T(8,128)(2,1)S(1)}, bf16[1,256,128]{2,1,0:T(8,128)(2,1)S(1)}, u32[]{:S(2)}, u32[]{:S(2)}) collective-permute-start(bf16[1,256,128]{2,1,0:T(8,128)(2,1)S(1)} %get-tuple-element.6), channel_id=1, source_target_pairs={{0,1},{1,2},{2,3},{3,4},{4,5},{5,6},{6,7},{7,8},{8,9},{9,10},{10,1... | collective-permute-start | bytes 196616 | tf_op jit(solution)/shard_map/ppermute | solution.py:72
  24.4 6.4 %collective-permute-start.1 = (bf16[1,256,128]{2,1,0:T(8,128)(2,1)S(1)}, bf16[1,256,128]{2,1,0:T(8,128)(2,1)S(1)}, u32[]{:S(2)}, u32[]{:S(2)}) collective-permute-start(bf16[1,256,128]{2,1,0:T(8,128)(2,1)S(1)} %get-tuple-element.5), channel_id=1, source_target_pairs={{1,0},{2,1},{3,2},{4,3},{5,4},{6,5},{7,6},{8,7},{9,8},{10,9},{11,1... | collective-permute-start | bytes 196616 | tf_op jit(solution)/shard_map/ppermute | solution.py:75
  30.8 0.0 copy-done.4
  30.9 0.0 copy-done.2
  30.9 0.0 copy-start.5
  30.9 0.0 copy-start.6
  30.9 97.2 %gather_fusion = f32[16384]{0:T(1024)S(1)} fusion(f32[128]{0:T(128)S(1)} %copy-done.2, s32[16384]{0:T(1024)S(1)} %fusion.39), kind=kCustom, calls=%fused_computation | custom fusion | bytes 196608 | tf_op jit(solution)/shard_map/gather | solution.py:84
  128.1 0.0 copy-done.5
  128.1 0.1 fusion.45
  128.2 0.0 copy-done
  128.2 0.0 copy-done.6
  128.2 2.9 %fusion.10 = f32[32,256,16]{1,2,0:T(8,128)S(1)} fusion(f32[32,64,256]{2,1,0:T(8,128)S(1)} %copy-done, s32[]{:T(128)S(6)} %select_n.17, f32[32,64]{1,0:T(8,128)S(1)} %fusion.45, s32[32,64]{1,0:T(8,128)S(1)} %copy-done.6), kind=kOutput, calls=%fused_computation.15 | convolution fusion | flops 101711872 | bytes 1605636 | tf_op jit(solution)/shard_map/cfs,cfq->csq/dot_general | solution.py:124
  131.1 0.0 all-to-all-done
  131.1 2.6 %reduce_sum.9 = bf16[16,32,128]{2,1,0:T(8,128)(2,1)S(1)} reduce(f32[16,16,32,128]{3,2,1,0:T(8,128)} %all-to-all-done, f32[]{:T(128)} %constant.11.clone.1), dimensions={0}, to_apply=%region_0.0 | reduce | flops 983040 | bytes 4325380 | tf_op jit(solution)/shard_map/reduce_sum | solution.py:20
  133.7 0.0 copy-start.3
  133.8 10.7 %all-gather.1 = bf16[64,16,128]{2,1,0:T(8,128)(2,1)S(1)} all-gather(bf16[16,16,128]{2,1,0:T(8,128)(2,1)S(1)} %get-tuple-element.8), channel_id=3, replica_groups=mesh['box_0'=4,'box_1'=2,'dir'=16] {'box_0'}, dimensions={0}, use_global_device_ids=true | all-gather | bytes 327680 | tf_op jit(solution)/shard_map/all_gather | solution.py:31
  144.5 5.8 %all_gather.15 = bf16[8,16,16,128]{3,2,1,0:T(8,128)(2,1)S(1)} all-gather(bf16[4,16,16,128]{3,2,1,0:T(8,128)(2,1)S(1)} %bitcast.102), channel_id=1, replica_groups=mesh['box_0'=4,'box_1'=2,'dir'=16] {'box_1'}, dimensions={0}, use_global_device_ids=true | all-gather | bytes 786432 | tf_op jit(solution)/shard_map/all_gather | solution.py:31
  150.4 1.9 all-gather
  152.3 11.2 %all_gather.13 = bf16[8,16,16,128]{3,2,1,0:T(8,128)(2,1)S(1)} all-gather(bf16[2,16,16,128]{3,2,1,0:T(8,128)(2,1)S(1)} %bitcast.103), channel_id=1, replica_groups=mesh['box_0'=4,'box_1'=2,'dir'=16] {'box_0'}, dimensions={0}, use_global_device_ids=true | all-gather | bytes 655360 | tf_op jit(solution)/shard_map/all_gather | solution.py:31
  163.5 0.1 maximum_bitcast_fusion
  163.6 0.1 copy.62
  163.7 0.8 convolution_bitcast_fusion.2
  164.6 0.5 convolution_convert_fusion
  165.1 1.7 broadcast_in_dim.36
  166.8 3.9 %all-to-all-start.1 = ((bf16[16,32,16,128]{3,2,1,0:T(8,128)(2,1)}), bf16[16,32,16,128]{3,2,1,0:T(8,128)(2,1)S(1)}, u32[]{:S(2)}, u32[]{:S(2)}) async-start(bf16[16,32,16,128]{3,2,1,0:T(8,128)(2,1)} %broadcast_in_dim.36), calls=%async_computation.1 | async-start | bytes 4194304 | tf_op jit(solution)/shard_map/all_to_all | solution.py:58
  170.7 0.0 copy-done.3
  170.7 11.5 %convolution_bitcast_fusion.1 = f32[128,256,128]{1,2,0:T(8,128)} fusion(bf16[128,256,128]{2,1,0:T(8,128)(2,1)} %param.10, bf16[3,256,256]{2,1,0:T(8,128)(2,1)S(1)} %copy-done.3), kind=kOutput, calls=%fused_computation.8 | convolution fusion | flops 2147483648 | bytes 25296896 | tf_op jit(solution)/shard_map/pr,lrt->lpt/dot_general | solution.py:149
  182.2 5.8 %convolution_bitcast_fusion = f32[128,256,128]{1,2,0:T(8,128)S(1)} fusion(bf16[128,256,128]{2,1,0:T(8,128)(2,1)} %param.10, bf16[3,256,256]{2,1,0:T(8,128)(2,1)S(1)} %copy-done.3), kind=kOutput, calls=%fused_computation.7 | convolution fusion | flops 2147483648 | bytes 25296896 | tf_op jit(solution)/shard_map/pr,lrt->lpt/dot_general | solution.py:152
  188.0 11.8 %slice.52 = f32[127,256,128]{1,2,0:T(8,128)} slice(f32[128,256,128]{1,2,0:T(8,128)} %convolution_bitcast_fusion.1), slice={[0:127], [0:256], [0:128]} | slice | bytes 33292288 | tf_op jit(solution)/shard_map/slice | solution.py:157
  199.9 6.0 %slice.53 = f32[127,256,128]{1,2,0:T(8,128)} slice(f32[128,256,128]{1,2,0:T(8,128)S(1)} %convolution_bitcast_fusion), slice={[1:128], [0:256], [0:128]} | slice | bytes 33292288 | tf_op jit(solution)/shard_map/slice | solution.py:158
  205.9 0.0 collective-permute-done
  205.9 0.2 convolution_bitcast_fusion.4
  206.1 0.0 collective-permute-done.1
  206.1 0.2 convolution_bitcast_fusion.3
  206.3 0.0 all-to-all-done.1
  206.3 0.6 copy.66
  206.9 1.3 fusion.18
  208.2 11.5 %fusion.4 = f32[2,128,64,256]{3,1,2,0:T(8,128)} fusion(bf16[64,256,256]{2,1,0:T(8,128)(2,1)} %param.19, bf16[2,256,128,1]{2,0,1,3:T(2,128)(2,1)S(1)} %fusion.18), kind=kOutput, calls=%fused_computation.9 | convolution fusion | flops 2147483648 | bytes 25296896 | tf_op jit(solution)/shard_map/spq,bqt->bspt/dot_general | solution.py:141
  219.7 0.0 copy-start.1
  219.7 23.8 %fusion.3 = bf16[128,256,128]{1,2,0:T(8,128)(2,1)} fusion(f32[127,256,128]{1,2,0:T(8,128)} %slice.52, f32[1,256,128]{1,2,0:T(8,128)S(1)} %convolution_bitcast_fusion.4, f32[1,256,128]{1,2,0:T(8,128)S(1)} %convolution_bitcast_fusion.3, f32[127,256,128]{1,2,0:T(8,128)} %slice.53, f32[2,128,64,256]{3,1,2,0:T(8,128)} %fusion.4, ...), kind=kOutput, calls=%fused_computation.5 | convolution fusion | flops 2181038080 | bytes 67240960 | tf_op jit(solution)/shard_map/pr,lrt->lpt/dot_general | solution.py:146
  243.5 11.9 %copy.69 = bf16[128,256,128]{2,1,0:T(8,128)(2,1)} copy(bf16[128,256,128]{1,2,0:T(8,128)(2,1)} %fusion.3) | data formatting | bytes 16777216 | tf_op jit(solution)/shard_map/convert_element_type | solution.py:164
  255.4 0.0 copy-done.1
  (6 shorter events, 0.1 us)
Async XLA Ops:
  0.0 128.2 %copy-start = (f32[32,64,256]{2,1,0:T(8,128)S(1)}, f32[32,64,256]{2,1,0:T(8,128)}, u32[]{:S(2)}) copy-start(f32[32,64,256]{2,1,0:T(8,128)} %param.17) | copy-start | bytes 6291460
  0.0 8.5 %copy-start.7 = (s32[128]{0:T(128)S(1)}, s32[128]{0:T(128)}, u32[]{:S(2)}) copy-start(s32[128]{0:T(128)} %param.11) | copy-start | bytes 1540
  8.3 22.5 %copy-start.4 = (s32[128,2]{0,1:T(2,128)S(1)}, s32[128,2]{0,1:T(2,128)}, u32[]{:S(2)}) copy-start(s32[128,2]{0,1:T(2,128)} %param.12) | copy-start | bytes 3076
  8.3 22.5 %copy-start.2 = (f32[128]{0:T(128)S(1)}, f32[128]{0:T(128)}, u32[]{:S(2)}) copy-start(f32[128]{0:T(128)} %param.18) | copy-start | bytes 1540
  12.7 118.4 %all-to-all-start = ((f32[16,16,32,128]{3,2,1,0:T(8,128)}), f32[16,16,32,128]{3,2,1,0:T(8,128)}, u32[]{:S(2)}, u32[]{:S(2)}) async-start(f32[16,16,32,128]{3,2,1,0:T(8,128)} %bitcast.97), calls=%async_computation | async-start | bytes 8388608 | tf_op jit(solution)/shard_map/all_to_all | solution.py:19
  21.2 184.7 %collective-permute-start = (bf16[1,256,128]{2,1,0:T(8,128)(2,1)S(1)}, bf16[1,256,128]{2,1,0:T(8,128)(2,1)S(1)}, u32[]{:S(2)}, u32[]{:S(2)}) collective-permute-start(bf16[1,256,128]{2,1,0:T(8,128)(2,1)S(1)} %get-tuple-element.6), channel_id=1, source_target_pairs={{0,1},{1,2},{2,3},{3,4},{4,5},{5,6},{6,7},{7,8},{8,9},{9,10},{10,1... | collective-permute-start | bytes 196616 | tf_op jit(solution)/shard_map/ppermute | solution.py:72
  24.4 181.7 %collective-permute-start.1 = (bf16[1,256,128]{2,1,0:T(8,128)(2,1)S(1)}, bf16[1,256,128]{2,1,0:T(8,128)(2,1)S(1)}, u32[]{:S(2)}, u32[]{:S(2)}) collective-permute-start(bf16[1,256,128]{2,1,0:T(8,128)(2,1)S(1)} %get-tuple-element.5), channel_id=1, source_target_pairs={{1,0},{2,1},{3,2},{4,3},{5,4},{6,5},{7,6},{8,7},{9,8},{10,9},{11,1... | collective-permute-start | bytes 196616 | tf_op jit(solution)/shard_map/ppermute | solution.py:75
  30.9 97.2 %copy-start.5 = (s32[32]{0:T(128)S(1)}, s32[32]{0:T(128)}, u32[]{:S(2)}) copy-start(s32[32]{0:T(128)} %param.16) | copy-start | bytes 388
  30.9 97.3 %copy-start.6 = (s32[32,64]{1,0:T(8,128)S(1)}, s32[32,64]{1,0:T(8,128)}, u32[]{:S(2)}) copy-start(s32[32,64]{1,0:T(8,128)} %param.15) | copy-start | bytes 24580
  133.7 36.9 %copy-start.3 = (bf16[3,256,256]{2,1,0:T(8,128)(2,1)S(1)}, bf16[3,256,256]{2,1,0:T(8,128)(2,1)}, u32[]{:S(2)}) copy-start(bf16[3,256,256]{2,1,0:T(8,128)(2,1)} %param.13) | copy-start | bytes 1179652
  166.8 39.6 %all-to-all-start.1 = ((bf16[16,32,16,128]{3,2,1,0:T(8,128)(2,1)}), bf16[16,32,16,128]{3,2,1,0:T(8,128)(2,1)S(1)}, u32[]{:S(2)}, u32[]{:S(2)}) async-start(bf16[16,32,16,128]{3,2,1,0:T(8,128)(2,1)} %broadcast_in_dim.36), calls=%async_computation.1 | async-start | bytes 4194304 | tf_op jit(solution)/shard_map/all_to_all | solution.py:58
  219.7 35.7 %copy-start.1 = (f32[32,64,256]{2,1,0:T(8,128)S(1)}, f32[32,64,256]{2,1,0:T(8,128)}, u32[]{:S(2)}) copy-start(f32[32,64,256]{2,1,0:T(8,128)} %param.17) | copy-start | bytes 6291460
where the time goes:
time: 257 us; the launch traced here: 255 us
  local copies, waits for them, and re-layouts  131 us (51%)
  matrix products  70.7 us (28%)
  blocking collectives  29.7 us (12%)
  starting transfers between devices  21.1 us (8%)
  other arithmetic  2.84 us (1%)
    gather x1, local copies, waits for them, and re-layouts, time_matrix(): kernel[jnp.clip(sample_lag, 0, length - 1)]  97.2 us
    all_gather x4, blocking collectives, all_blocks(): tiles = lax.all_gather(tiles, axes[k], axis=0, tiled=True)  29.7 us
    dot_general x1, matrix products, per_device(): jnp.einsum('pr,lrt->lpt', near_blocks[0], currents, preferred_element_typ...  23.8 us
    convert_element_type x1, local copies, waits for them, and re-layouts, per_device(): return (near_field + far_field).astype(jnp.bfloat16)  11.9 us
    slice x1, local copies, waits for them, and re-layouts, per_device(): before_term = jnp.concatenate([before_rim[None], before_all[:-1]], axis=0)  11.8 us
    dot_general x1, matrix products, per_device(): jnp.einsum('spq,bqt->bspt', map_block, selected, preferred_element_type=j...  11.5 us
    dot_general x1, matrix products, per_device(): jnp.einsum('pr,lrt->lpt', near_blocks[1], currents, preferred_element_typ...  11.5 us
    dot_general x1, matrix products, per_device(): jnp.einsum('sqp,bspt->bqt', map_block, leaf_runs, preferred_element_type=...  8.31 us
  transfers between devices with their start and end apart: 4, of which 0 were waited for; matrix products, arithmetic and copies ran while one was open for 56% of the time, Pallas kernels for 0%

commit v1 on v0

v1 whole, which is shorter than its diff:
```python
import jax
import jax.numpy as jnp
from jax import lax
from jax.experimental import pallas as pl
from jax.experimental.pallas import tpu as pltpu
from jax.sharding import PartitionSpec as P

AXES = ("box", "dir")
RUN = 64
SLOTS = 64
CHUNKS = 8
CHUNK = RUN // CHUNKS
UNK = 256
TIME = 128
DEVS = 128
ROWS = 8
F32, BF16 = jnp.float32, jnp.bfloat16
MIB = 1 << 20


def whole(space=pltpu.VMEM):
    return pl.BlockSpec(memory_space=space)


def params(mib):
    return pltpu.CompilerParams(vmem_limit_bytes=mib * MIB)


def aggregate(parent, counts, cur_hbm, agg_hbm, coef_hbm, boxes, cur, sent, maps, coef, wide, total, sems, coef_sems):
    cur_copies, map_copies = [], []
    for k in range(CHUNKS):
        for run in range(2):
            part = pl.ds(run * RUN + k * CHUNK, CHUNK)
            cur_copies.append(pltpu.make_async_copy(cur_hbm.at[part], cur.at[part], sems.at[run, k]))
        part = pl.ds(k * CHUNK, CHUNK)
        map_copies.append(pltpu.make_async_copy(agg_hbm.at[part], maps.at[part], sems.at[2, k]))
    own = [lax.rem(parent[run * RUN], boxes.shape[0]) for run in range(2)]
    coef_copies = [
        pltpu.make_async_copy(coef_hbm.at[own[run]], coef.at[run], coef_sems.at[run]) for run in range(2)
    ]
    for k in range(CHUNKS):
        cur_copies[2 * k].start()
        cur_copies[2 * k + 1].start()
        map_copies[k].start()
        if k == 0:
            for copy in coef_copies:
                copy.start()
    for copy in coef_copies:
        copy.wait()
    row = lax.broadcasted_iota(jnp.int32, (2 * SLOTS, UNK), 0)
    used = row < jnp.where(row < SLOTS, counts[own[0]], SLOTS + counts[own[1]])
    turned = jnp.where(used, coef[...].reshape(2 * SLOTS, UNK), 0.0).T
    for half in range(2):
        wide[pl.ds(4 + half, DEVS, stride=ROWS), :] = turned[half * DEVS : (half + 1) * DEVS]
    listed = jnp.concatenate([boxes[pl.ds(own[run], 1), :] for run in range(2)], axis=1)
    wide[pl.ds(6, DEVS, stride=ROWS), :] = jnp.broadcast_to(listed.astype(F32), (DEVS, 2 * SLOTS))
    lane = lax.broadcasted_iota(jnp.int32, (DEVS, 2 * SLOTS), 1)
    wide[pl.ds(7, DEVS, stride=ROWS), :] = jnp.where(lane < SLOTS, parent[0], parent[RUN]).astype(F32)

    for k in range(CHUNKS):
        cur_copies[2 * k].wait()
        cur_copies[2 * k + 1].wait()
        map_copies[k].wait()
        left = jnp.concatenate([maps[k * CHUNK + i] for i in range(CHUNK)], axis=1)
        right = jnp.concatenate(
            [cur[pl.ds(run * RUN + k * CHUNK, CHUNK)].reshape(CHUNK * UNK, TIME) for run in range(2)], axis=1
        )
        part = jnp.dot(left, right, preferred_element_type=F32)
        total[...] = part if k == 0 else total[...] + part
    for half in range(2):
        for run in range(2):
            wide[pl.ds(2 * half + run, DEVS, stride=ROWS), :] = total[
                half * DEVS : (half + 1) * DEVS, run * TIME : (run + 1) * TIME
            ]
    sent[...] = wide[...].astype(BF16)


def near(links, blocks, cur, low, high, dis_hbm, out, dis, sems):
    copies = [
        pltpu.make_async_copy(dis_hbm.at[pl.ds(k * CHUNK, CHUNK)], dis.at[pl.ds(k * CHUNK, CHUNK)], sems.at[k])
        for k in range(CHUNKS)
    ]
    for copy in copies:
        copy.start()
    left = jnp.concatenate([blocks[k] for k in range(3)], axis=1)

    def masked(leaf, side, value):
        return value * links[leaf, side].astype(F32).astype(BF16)

    def pair(i, before, after):
        own = jnp.concatenate([cur[i], cur[RUN + i]], axis=1)
        previous = jnp.concatenate(
            [masked(i, 0, before), masked(RUN + i, 0, cur[RUN + i - 1])], axis=1
        )
        following = jnp.concatenate([masked(i, 1, cur[i + 1]), masked(RUN + i, 1, after)], axis=1)
        right = jnp.concatenate([own, previous, following], axis=0)
        done = jnp.dot(left, right, preferred_element_type=F32)
        out[i] = done[:, :TIME]
        out[RUN + i] = done[:, TIME:]

    pair(0, low[...], cur[RUN + 1])

    @pl.loop(1, RUN - 1)
    def _(i):
        pair(i, cur[i - 1], cur[RUN + i + 1])

    pair(RUN - 1, cur[RUN - 2], high[...])
    for copy in copies:
        copy.wait()


def split(value):
    big = value.astype(BF16)
    return big, (value - big.astype(F32)).astype(BF16)


def translate(got, kernel, out, wide, tall):
    wide[...] = got[...].astype(F32)
    parents = wide[pl.ds(7, DEVS, stride=ROWS), :].T
    source = [parents[0:1], parents[SLOTS : SLOTS + 1]]
    coef = [wide[pl.ds(4 + half, DEVS, stride=ROWS), :] for half in range(2)]
    listed = wide[pl.ds(6, DEVS, stride=ROWS), :]
    lag = jnp.broadcast_to(kernel[...], (TIME, TIME))
    lag = pltpu.roll(lag, 0, 1, stride=1, stride_axis=0)
    row = lax.broadcasted_iota(jnp.int32, (TIME, TIME), 0)
    column = lax.broadcasted_iota(jnp.int32, (TIME, TIME), 1)
    lag_big, lag_rest = split(jnp.where(column >= row, lag, 0.0))
    rows = []
    for run in range(2):
        for block in range(DEVS // 8):
            at = slice(block * 8, block * 8 + 8)
            weight = [[jnp.zeros((8, DEVS), F32) for _ in range(2)] for _ in range(2)]
            for slot in range(run * SLOTS, (run + 1) * SLOTS):
                name = listed[at, slot : slot + 1]
                for side in range(2):
                    here = name == source[side]
                    for half in range(2):
                        weight[half][side] = weight[half][side] + jnp.where(
                            here, coef[half][at, slot : slot + 1], 0.0
                        )
            rows.append([jnp.concatenate(weight[half], axis=1) for half in range(2)])
    for half in range(2):
        rays = jnp.concatenate(
            [wide[pl.ds(2 * half + run, DEVS, stride=ROWS), :] for run in range(2)], axis=0
        ).astype(BF16)
        big, rest = split(jnp.concatenate([r[half] for r in rows], axis=0))
        far = jnp.dot(big, rays, preferred_element_type=F32) + jnp.dot(rest, rays, preferred_element_type=F32)
        far_big, far_rest = split(far)
        done = (
            jnp.dot(far_big, lag_big, preferred_element_type=F32)
            + jnp.dot(far_rest, lag_big, preferred_element_type=F32)
            + jnp.dot(far_big, lag_rest, preferred_element_type=F32)
        )
        for run in range(2):
            tall[pl.ds(2 * half + run, DEVS, stride=4), :] = done[run * DEVS : (run + 1) * DEVS]
    out[...] = tall[...].astype(BF16)


def disaggregate(got, near_field, dis, out, tall, incoming):
    step = pl.program_id(0)

    @pl.when(step == 0)
    def _():
        tall[...] = got[...].astype(F32)
        for half in range(2):
            for run in range(2):
                incoming[half * DEVS : (half + 1) * DEVS, run * TIME : (run + 1) * TIME] = tall[
                    pl.ds(2 * half + run, DEVS, stride=4), :
                ].astype(BF16)

    for i in range(CHUNK):
        leaf = step * CHUNK + i
        far = jnp.dot(dis[leaf], incoming[...], preferred_element_type=F32)
        for run in range(2):
            out[run, i] = (near_field[run * RUN + leaf] + far[:, run * TIME : (run + 1) * TIME]).astype(BF16)


def per_device(
    currents,
    leaf_parent,
    near_links,
    near_blocks,
    aggregate_maps,
    far_boxes,
    far_counts,
    translate_coef,
    time_kernel,
    disaggregate_maps,
):
    leaves = 2 * RUN
    low = lax.ppermute(currents[leaves - 1], AXES, [(i, i + 1) for i in range(DEVS - 1)])
    high = lax.ppermute(currents[0], AXES, [(i + 1, i) for i in range(DEVS - 1)])
    held, sent = pl.pallas_call(
        aggregate,
        out_shape=(
            pltpu.VMEM((leaves, UNK, TIME), BF16),
            jax.ShapeDtypeStruct((DEVS * ROWS, TIME), BF16),
        ),
        in_specs=[
            whole(pltpu.SMEM),
            whole(pltpu.SMEM),
            whole(pl.ANY),
            whole(pl.ANY),
            whole(pl.ANY),
            whole(),
        ],
        out_specs=(whole(), whole()),
        scratch_shapes=[
            pltpu.VMEM((RUN, UNK, UNK), BF16),
            pltpu.VMEM((2, SLOTS, UNK), F32),
            pltpu.VMEM((DEVS * ROWS, TIME), F32),
            pltpu.VMEM((UNK, UNK), F32),
            pltpu.SemaphoreType.DMA((3, CHUNKS)),
            pltpu.SemaphoreType.DMA((2,)),
        ],
        compiler_params=params(20),
        cost_estimate=pl.CostEstimate(flops=2 << 30, bytes_accessed=17 * MIB, transcendentals=0),
        name="aggregate",
    )(leaf_parent, far_counts, currents, aggregate_maps, translate_coef, far_boxes)
    arrived = lax.all_to_all(sent.reshape(DEVS, ROWS, TIME), AXES, 0, 0, tiled=True)
    near_field, dis = pl.pallas_call(
        near,
        out_shape=(
            pltpu.VMEM((leaves, UNK, TIME), F32),
            pltpu.VMEM((RUN, UNK, UNK), BF16),
        ),
        in_specs=[whole(pltpu.SMEM), whole(), whole(), whole(), whole(), whole(pl.ANY)],
        out_specs=(whole(), whole()),
        scratch_shapes=[pltpu.SemaphoreType.DMA((CHUNKS,))],
        compiler_params=params(12),
        cost_estimate=pl.CostEstimate(flops=6 << 30, bytes_accessed=17 * MIB, transcendentals=0),
        name="near",
    )(
        near_links,
        near_blocks,
        pltpu.with_memory_space_constraint(held, pltpu.VMEM),
        low,
        high,
        disaggregate_maps,
    )
    incoming = pl.pallas_call(
        translate,
        out_shape=jax.ShapeDtypeStruct((DEVS * 4, TIME), BF16),
        in_specs=[whole(), whole()],
        out_specs=whole(),
        scratch_shapes=[pltpu.VMEM((DEVS * ROWS, TIME), F32), pltpu.VMEM((DEVS * 4, TIME), F32)],
        compiler_params=params(12),
        cost_estimate=pl.CostEstimate(flops=1 << 28, bytes_accessed=MIB, transcendentals=0),
        name="translate",
    )(arrived.reshape(DEVS * ROWS, TIME), time_kernel.reshape(1, TIME))
    returned = lax.all_to_all(incoming.reshape(DEVS, 4, TIME), AXES, 0, 0, tiled=True)
    field = pl.pallas_call(
        disaggregate,
        grid=(CHUNKS,),
        out_shape=jax.ShapeDtypeStruct((2, RUN, UNK, TIME), BF16),
        in_specs=[whole(), whole(), whole()],
        out_specs=pl.BlockSpec((2, CHUNK, UNK, TIME), lambda i: (0, i, 0, 0)),
        scratch_shapes=[pltpu.VMEM((DEVS * 4, TIME), F32), pltpu.VMEM((UNK, UNK), BF16)],
        compiler_params=params(12),
        cost_estimate=pl.CostEstimate(flops=2 << 30, bytes_accessed=9 * MIB, transcendentals=0),
        name="disaggregate",
    )(
        returned.reshape(DEVS * 4, TIME),
        pltpu.with_memory_space_constraint(near_field, pltpu.VMEM),
        pltpu.with_memory_space_constraint(dis, pltpu.VMEM),
    )
    return field.reshape(leaves, UNK, TIME)


def solution(mesh):
    in_specs = (
        P(AXES, None, None),
        P(AXES),
        P(AXES, None),
        P(),
        P(),
        P("box", None),
        P("box"),
        P("box", None, None),
        P(),
        P(),
    )
    return jax.shard_map(
        per_device, mesh=mesh, in_specs=in_specs, out_specs=P(AXES, None, None), check_vma=False
    )
```

time: 257 us -> 116 us (0.45)
  local copies, waits for them, and re-layouts: 131 us -> 39.8 us
  matrix products: 70.7 us -> 0 us
  Pallas kernels: 0 us -> 45 us
  blocking collectives: 29.7 us -> 0 us
  starting transfers between devices: 21.1 us -> 29.4 us
  other arithmetic: 2.84 us -> 0 us
    gather x1 -> x0, local copies, waits for them, and re-layouts: 97.2 us -> none  [time_matrix(): kernel[jnp.clip(sample_lag, 0, length - 1)]]
    dot_general x12 -> x0, matrix products: 70.7 us -> none  [the longest x1 23.8 us: per_device(): jnp.einsum('pr,lrt->lpt', near_blocks[0], currents, preferred_element_typ...]
    pallas_call x0 -> x4, Pallas kernels: none -> 45 us  [the longest x1 19.9 us: per_device(): pl.pallas_call(near, out_shape=(pltpu.VMEM((leaves, UNK, TIME), F32), plt...]
    unnamed x16 -> x33, local copies, waits for them, and re-layouts: 0.04 us -> 38.9 us
    all_gather x4 -> x0, blocking collectives: 29.7 us -> none  [all_blocks(): tiles = lax.all_gather(tiles, axes[k], axis=0, tiled=True)]
    slice x5 -> x0, local copies, waits for them, and re-layouts: 18.9 us -> none  [the longest x1 11.8 us: per_device(): before_term = jnp.concatenate([before_rim[None], before_all[:-1]], axis=0)]
    convert_element_type x1 -> x0, local copies, waits for them, and re-layouts: 11.9 us -> none  [per_device(): return (near_field + far_field).astype(jnp.bfloat16)]
    all_to_all x2, starting transfers between devices: 11.5 us -> 20.3 us  [the longest x1 11.5 us: per_device(): lax.all_to_all(sent.reshape(DEVS, ROWS, TIME), AXES, 0, 0, tiled=True)]
  transfers between devices with their start and end apart: 4 -> 4, of which waited for: 0 -> 1; matrix products, arithmetic and copies ran while one was open for 56% -> 1% of each run, Pallas kernels for 0% -> 27%
where the time goes in v1:
time: 116 us; the launch traced here: 115 us
  Pallas kernels  45 us (39%)
  local copies, waits for them, and re-layouts  39.8 us (34%)
  starting transfers between devices  29.4 us (25%)
    unnamed x33, local copies, waits for them, and re-layouts  38.9 us
    pallas_call x1, Pallas kernels, per_device(): pl.pallas_call(near, out_shape=(pltpu.VMEM((leaves, UNK, TIME), F32), plt...  19.9 us
    all_to_all x1, starting transfers between devices, per_device(): lax.all_to_all(sent.reshape(DEVS, ROWS, TIME), AXES, 0, 0, tiled=True)  11.5 us
    pallas_call x1, Pallas kernels, per_device(): pl.pallas_call(translate, out_shape=jax.ShapeDtypeStruct((DEVS * 4, TIME)...  11.2 us
    all_to_all x1, starting transfers between devices, per_device(): lax.all_to_all(incoming.reshape(DEVS, 4, TIME), AXES, 0, 0, tiled=True)  8.85 us
    pallas_call x1, Pallas kernels, per_device(): pl.pallas_call(aggregate, out_shape=(pltpu.VMEM((leaves, UNK, TIME), BF16...  7.81 us
    ppermute x1, starting transfers between devices, per_device(): lax.ppermute(currents[0], AXES, [(i + 1, i) for i in range(DEVS - 1)])  6.96 us
    pallas_call x1, Pallas kernels, per_device(): pl.pallas_call(disaggregate, grid=(CHUNKS,), out_shape=jax.ShapeDtypeStru...  6.13 us
  transfers between devices with their start and end apart: 4, of which 1 were waited for; matrix products, arithmetic and copies ran while one was open for 1% of the time, Pallas kernels for 27%

profile of v1, /device:TPU:1, one launch (start us, length us, event | category | flops | bytes accessed | tf_op | source)
XLA Modules:
  0.0 115.4 jit_solution(245923916989149975)
XLA Ops:
  0.0 0.0 copy-start.2
  0.0 3.4 %copy-done.2 = bf16[128,256,128]{2,1,0:T(8,128)(2,1)S(1)} copy-done((bf16[128,256,128]{2,1,0:T(8,128)(2,1)S(1)}, bf16[128,256,128]{2,1,0:T(8,128)(2,1)}, u32[]{:S(2)}) %copy-start.2) | copy-done | bytes 8388632
  3.4 0.0 copy-start.3
  3.4 3.4 %copy-done.3 = bf16[64,256,256]{2,1,0:T(8,128)(2,1)S(1)} copy-done((bf16[64,256,256]{2,1,0:T(8,128)(2,1)S(1)}, bf16[64,256,256]{2,1,0:T(8,128)(2,1)}, u32[]{:S(2)}) %copy-start.3) | copy-done | bytes 8388632
  6.8 0.0 copy-start.6
  6.8 1.6 %copy-done.6 = f32[32,64,256]{2,1,0:T(8,128)S(1)} copy-done((f32[32,64,256]{2,1,0:T(8,128)S(1)}, f32[32,64,256]{2,1,0:T(8,128)}, u32[]{:S(2)}) %copy-start.6) | copy-done | bytes 2097176
  8.4 0.0 copy-start.7
  8.4 0.7 copy-done.7
  9.1 0.0 copy-start.8
  9.1 0.7 copy-done.8
  9.7 0.0 copy-start.9
  9.7 0.7 copy-done.9
  10.4 0.0 copy-start.15
  10.4 0.0 copy-start.14
  10.4 0.0 copy-start.13
  10.4 7.8 %aggregate.1 = (bf16[128,256,128]{2,1,0:T(8,128)(2,1)S(1)}, bf16[1024,128]{1,0:T(8,128)(2,1)}) custom-call(s32[128]{0:T(128)S(1)} %copy-done.8, s32[32]{0:T(128)S(1)} %copy-done.9, bf16[128,256,128]{2,1,0:T(8,128)(2,1)S(1)} %copy-done.2, bf16[64,256,256]{2,1,0:T(8,128)(2,1)S(1)} %copy-done.3, f32[32,64,256]{2,1,0:T(8,128)S(1)} %copy-done.6, ...), custom_call_target="tpu_custom_call" | custom-call | flops 2147483648 | bytes 17825792 | tf_op jit(solution)/shard_map/aggregate/pallas_call | solution.py:193
  18.2 0.0 copy-start.11
  18.2 3.4 %copy-done.11 = bf16[128,256,128]{2,1,0:T(8,128)(2,1)} copy-done((bf16[128,256,128]{2,1,0:T(8,128)(2,1)}, bf16[128,256,128]{2,1,0:T(8,128)(2,1)S(1)}, u32[]{:S(2)}) %copy-start.11) | copy-done | bytes 8388632
  21.6 11.5 %all-to-all-start = ((bf16[128,8,128]{2,1,0:T(8,128)(2,1)}), bf16[128,8,128]{2,1,0:T(8,128)(2,1)S(1)}, u32[]{:S(2)}, u32[]{:S(2)}) async-start(bf16[128,8,128]{2,1,0:T(8,128)(2,1)} %bitcast), calls=%async_computation | async-start | bytes 524288 | tf_op jit(solution)/shard_map/all_to_all | solution.py:220
  33.1 0.9 slice_bitcast_fusion
  34.0 7.0 %collective-permute-start.1 = (bf16[256,128]{1,0:T(8,128)(2,1)S(1)}, bf16[256,128]{1,0:T(8,128)(2,1)S(1)}, u32[]{:S(2)}, u32[]{:S(2)}) collective-permute-start(bf16[256,128]{1,0:T(8,128)(2,1)S(1)} %get-tuple-element.13), channel_id=1, source_target_pairs={{1,0},{2,1},{3,2},{4,3},{5,4},{6,5},{7,6},{8,7},{9,8},{10,9},{11,1... | collective-permute-start | bytes 196616 | tf_op jit(solution)/shard_map/ppermute | solution.py:192
  41.0 2.1 %collective-permute-start = (bf16[256,128]{1,0:T(8,128)(2,1)S(1)}, bf16[256,128]{1,0:T(8,128)(2,1)S(1)}, u32[]{:S(2)}, u32[]{:S(2)}) collective-permute-start(bf16[256,128]{1,0:T(8,128)(2,1)S(1)} %get-tuple-element.14), channel_id=1, source_target_pairs={{0,1},{1,2},{2,3},{3,4},{4,5},{5,6},{6,7},{7,8},{8,9},{9,10},{10,1... | collective-permute-start | bytes 196616 | tf_op jit(solution)/shard_map/ppermute | solution.py:191
  43.1 0.0 copy-done.15
  43.1 0.1 copy.11.links
  43.2 1.1 all-to-all-done
  44.3 0.0 copy-done.14
  44.3 11.2 %translate.1 = bf16[512,128]{1,0:T(8,128)(2,1)} custom-call(bf16[1024,128]{1,0:T(8,128)(2,1)S(1)} %bitcast.11, f32[1,128]{1,0:T(1,128)S(1)} %bitcast.12), custom_call_target="tpu_custom_call" | custom-call | flops 268435456 | bytes 1048576 | tf_op jit(solution)/shard_map/translate/pallas_call | solution.py:241
  55.4 8.8 %all-to-all-start.1 = ((bf16[128,4,128]{2,1,0:T(4,128)(2,1)}), bf16[128,4,128]{2,1,0:T(4,128)(2,1)S(1)}, u32[]{:S(2)}, u32[]{:S(2)}) async-start(bf16[128,4,128]{2,1,0:T(4,128)(2,1)} %bitcast.3), calls=%async_computation.1 | async-start | bytes 262144 | tf_op jit(solution)/shard_map/all_to_all | solution.py:251
  64.3 0.0 collective-permute-done.1.high
  64.3 0.0 collective-permute-done.low
  64.3 0.0 copy-done.13
  64.3 0.0 copy-start.10
  64.3 3.4 %copy-done.10 = bf16[64,256,256]{2,1,0:T(8,128)(2,1)S(1)} copy-done((bf16[64,256,256]{2,1,0:T(8,128)(2,1)S(1)}, bf16[64,256,256]{2,1,0:T(8,128)(2,1)}, u32[]{:S(2)}) %copy-start.10) | copy-done | bytes 8388632
  67.7 0.0 copy-start.12
  67.7 3.4 %copy-done.12 = bf16[128,256,128]{2,1,0:T(8,128)(2,1)S(1)} copy-done((bf16[128,256,128]{2,1,0:T(8,128)(2,1)S(1)}, bf16[128,256,128]{2,1,0:T(8,128)(2,1)}, u32[]{:S(2)}) %copy-start.12) | copy-done | bytes 8388632
  71.1 19.9 %near.1 = (f32[128,256,128]{2,1,0:T(8,128)S(1)}, bf16[64,256,256]{2,1,0:T(8,128)(2,1)S(1)}) custom-call(s32[128,2]{1,0:T(8,128)S(1)} %copy.11.links, bf16[3,256,256]{2,1,0:T(8,128)(2,1)S(1)} %copy-done.13, bf16[128,256,128]{2,1,0:T(8,128)(2,1)S(1)} %copy-done.12, bf16[256,128]{1,0:T(8,128)(2,1)S(1)} %collective-permute-done.low, ...), custom_call_target="tpu_custom_call" | custom-call | flops 6442450944 | bytes 17825792 | tf_op jit(solution)/shard_map/near/pallas_call | solution.py:221
  91.0 0.0 copy-start
  91.0 5.7 %copy-done = f32[128,256,128]{2,1,0:T(8,128)} copy-done((f32[128,256,128]{2,1,0:T(8,128)}, f32[128,256,128]{2,1,0:T(8,128)S(1)}, u32[]{:S(2)}) %copy-start) | copy-done | bytes 16777240
  96.7 0.0 copy-start.4
  96.7 3.4 %copy-done.4 = bf16[64,256,256]{2,1,0:T(8,128)(2,1)} copy-done((bf16[64,256,256]{2,1,0:T(8,128)(2,1)}, bf16[64,256,256]{2,1,0:T(8,128)(2,1)S(1)}, u32[]{:S(2)}) %copy-start.4) | copy-done | bytes 8388632
  100.1 0.0 all-to-all-done.1
  100.1 0.0 copy-start.1
  100.1 5.8 %copy-done.1 = f32[128,256,128]{2,1,0:T(8,128)S(1)} copy-done((f32[128,256,128]{2,1,0:T(8,128)S(1)}, f32[128,256,128]{2,1,0:T(8,128)}, u32[]{:S(2)}) %copy-start.1) | copy-done | bytes 16777240
  105.9 0.0 copy-start.5
  105.9 3.4 %copy-done.5 = bf16[64,256,256]{2,1,0:T(8,128)(2,1)S(1)} copy-done((bf16[64,256,256]{2,1,0:T(8,128)(2,1)S(1)}, bf16[64,256,256]{2,1,0:T(8,128)(2,1)}, u32[]{:S(2)}) %copy-start.5) | copy-done | bytes 8388632
  109.3 6.1 %disaggregate.1 = bf16[2,64,256,128]{3,2,1,0:T(8,128)(2,1)} custom-call(bf16[512,128]{1,0:T(8,128)(2,1)S(1)} %bitcast.10, f32[128,256,128]{2,1,0:T(8,128)S(1)} %copy-done.1, bf16[64,256,256]{2,1,0:T(8,128)(2,1)S(1)} %copy-done.5), custom_call_target="tpu_custom_call" | custom-call | flops 2147483648 | bytes 9437184 | tf_op jit(solution)/shard_map/disaggregate/pallas_call | solution.py:252
Async XLA Ops:
  0.0 3.4 %copy-start.2 = (bf16[128,256,128]{2,1,0:T(8,128)(2,1)S(1)}, bf16[128,256,128]{2,1,0:T(8,128)(2,1)}, u32[]{:S(2)}) copy-start(bf16[128,256,128]{2,1,0:T(8,128)(2,1)} %cur_hbm.1) | copy-start | bytes 25165828
  3.4 3.4 %copy-start.3 = (bf16[64,256,256]{2,1,0:T(8,128)(2,1)S(1)}, bf16[64,256,256]{2,1,0:T(8,128)(2,1)}, u32[]{:S(2)}) copy-start(bf16[64,256,256]{2,1,0:T(8,128)(2,1)} %agg_hbm.1) | copy-start | bytes 25165828
  6.8 1.6 %copy-start.6 = (f32[32,64,256]{2,1,0:T(8,128)S(1)}, f32[32,64,256]{2,1,0:T(8,128)}, u32[]{:S(2)}) copy-start(f32[32,64,256]{2,1,0:T(8,128)} %coef_hbm.1) | copy-start | bytes 6291460
  8.4 0.7 copy-start.7
  9.1 0.7 copy-start.8
  9.7 0.7 copy-start.9
  10.4 32.7 %copy-start.15 = (s32[128,2]{0,1:T(2,128)S(1)}, s32[128,2]{0,1:T(2,128)}, u32[]{:S(2)}) copy-start(s32[128,2]{0,1:T(2,128)} %param.12) | copy-start | bytes 3076
  10.4 33.9 %copy-start.14 = (f32[128]{0:T(128)S(1)}, f32[128]{0:T(128)}, u32[]{:S(2)}) copy-start(f32[128]{0:T(128)} %param.18) | copy-start | bytes 1540
  10.4 53.9 %copy-start.13 = (bf16[3,256,256]{2,1,0:T(8,128)(2,1)S(1)}, bf16[3,256,256]{2,1,0:T(8,128)(2,1)}, u32[]{:S(2)}) copy-start(bf16[3,256,256]{2,1,0:T(8,128)(2,1)} %blocks.1) | copy-start | bytes 1179652
  18.2 3.4 %copy-start.11 = (bf16[128,256,128]{2,1,0:T(8,128)(2,1)}, bf16[128,256,128]{2,1,0:T(8,128)(2,1)S(1)}, u32[]{:S(2)}) copy-start(bf16[128,256,128]{2,1,0:T(8,128)(2,1)S(1)} %get-tuple-element.10.cur) | copy-start | bytes 25165828
  21.6 22.7 %all-to-all-start = ((bf16[128,8,128]{2,1,0:T(8,128)(2,1)}), bf16[128,8,128]{2,1,0:T(8,128)(2,1)S(1)}, u32[]{:S(2)}, u32[]{:S(2)}) async-start(bf16[128,8,128]{2,1,0:T(8,128)(2,1)} %bitcast), calls=%async_computation | async-start | bytes 524288 | tf_op jit(solution)/shard_map/all_to_all | solution.py:220
  34.0 30.3 %collective-permute-start.1 = (bf16[256,128]{1,0:T(8,128)(2,1)S(1)}, bf16[256,128]{1,0:T(8,128)(2,1)S(1)}, u32[]{:S(2)}, u32[]{:S(2)}) collective-permute-start(bf16[256,128]{1,0:T(8,128)(2,1)S(1)} %get-tuple-element.13), channel_id=1, source_target_pairs={{1,0},{2,1},{3,2},{4,3},{5,4},{6,5},{7,6},{8,7},{9,8},{10,9},{11,1... | collective-permute-start | bytes 196616 | tf_op jit(solution)/shard_map/ppermute | solution.py:192
  41.0 23.3 %collective-permute-start = (bf16[256,128]{1,0:T(8,128)(2,1)S(1)}, bf16[256,128]{1,0:T(8,128)(2,1)S(1)}, u32[]{:S(2)}, u32[]{:S(2)}) collective-permute-start(bf16[256,128]{1,0:T(8,128)(2,1)S(1)} %get-tuple-element.14), channel_id=1, source_target_pairs={{0,1},{1,2},{2,3},{3,4},{4,5},{5,6},{6,7},{7,8},{8,9},{9,10},{10,1... | collective-permute-start | bytes 196616 | tf_op jit(solution)/shard_map/ppermute | solution.py:191
  55.4 44.7 %all-to-all-start.1 = ((bf16[128,4,128]{2,1,0:T(4,128)(2,1)}), bf16[128,4,128]{2,1,0:T(4,128)(2,1)S(1)}, u32[]{:S(2)}, u32[]{:S(2)}) async-start(bf16[128,4,128]{2,1,0:T(4,128)(2,1)} %bitcast.3), calls=%async_computation.1 | async-start | bytes 262144 | tf_op jit(solution)/shard_map/all_to_all | solution.py:251
  64.3 3.4 %copy-start.10 = (bf16[64,256,256]{2,1,0:T(8,128)(2,1)S(1)}, bf16[64,256,256]{2,1,0:T(8,128)(2,1)}, u32[]{:S(2)}) copy-start(bf16[64,256,256]{2,1,0:T(8,128)(2,1)} %dis_hbm.1) | copy-start | bytes 25165828
  67.7 3.4 %copy-start.12 = (bf16[128,256,128]{2,1,0:T(8,128)(2,1)S(1)}, bf16[128,256,128]{2,1,0:T(8,128)(2,1)}, u32[]{:S(2)}) copy-start(bf16[128,256,128]{2,1,0:T(8,128)(2,1)} %copy-done.11) | copy-start | bytes 25165828
  91.0 5.7 %copy-start = (f32[128,256,128]{2,1,0:T(8,128)}, f32[128,256,128]{2,1,0:T(8,128)S(1)}, u32[]{:S(2)}) copy-start(f32[128,256,128]{2,1,0:T(8,128)S(1)} %get-tuple-element.11.near_field) | copy-start | bytes 50331652
  96.7 3.4 %copy-start.4 = (bf16[64,256,256]{2,1,0:T(8,128)(2,1)}, bf16[64,256,256]{2,1,0:T(8,128)(2,1)S(1)}, u32[]{:S(2)}) copy-start(bf16[64,256,256]{2,1,0:T(8,128)(2,1)S(1)} %get-tuple-element.12.dis) | copy-start | bytes 25165828
  100.1 5.8 %copy-start.1 = (f32[128,256,128]{2,1,0:T(8,128)S(1)}, f32[128,256,128]{2,1,0:T(8,128)}, u32[]{:S(2)}) copy-start(f32[128,256,128]{2,1,0:T(8,128)} %copy-done) | copy-start | bytes 50331652
  105.9 3.4 %copy-start.5 = (bf16[64,256,256]{2,1,0:T(8,128)(2,1)S(1)}, bf16[64,256,256]{2,1,0:T(8,128)(2,1)}, u32[]{:S(2)}) copy-start(bf16[64,256,256]{2,1,0:T(8,128)(2,1)} %copy-done.4) | copy-start | bytes 25165828

commit v2 on v1

v2 whole, which is shorter than its diff:
```python
import jax
import jax.numpy as jnp
from jax import lax
from jax.experimental import pallas as pl
from jax.experimental.pallas import tpu as pltpu
from jax.sharding import PartitionSpec as P

AXES = ("box", "dir")
RUN = 64
SLOTS = 64
CHUNKS = 8
CHUNK = RUN // CHUNKS
EARLY = 32
EDGE = (RUN - EARLY) // 2
STEP = 8
AHEAD = 3
UNK = 256
TIME = 128
DEVS = 128
ROWS = 16
F32, BF16 = jnp.float32, jnp.bfloat16
NEAR = BF16
MIB = 1 << 20


def whole(space=pltpu.VMEM):
    return pl.BlockSpec(memory_space=space)


def params(mib):
    return pltpu.CompilerParams(vmem_limit_bytes=mib * MIB)


def in_hbm(*arrays):
    return [pltpu.with_memory_space_constraint(array, pltpu.HBM) for array in arrays]


def split(value):
    big = value.astype(BF16)
    return big, (value - big.astype(F32)).astype(BF16)


def aggregate(
    parent_hbm, counts_hbm, boxes_hbm, coef_hbm, cur_hbm, agg_hbm, sent,
    cur, maps, coef, boxes, parent, counts, wide, total, sems, small_sems,
):
    small = [
        pltpu.make_async_copy(source, target, small_sems.at[k])
        for k, (source, target) in enumerate(
            ((parent_hbm, parent), (counts_hbm, counts), (boxes_hbm, boxes))
        )
    ]
    for copy in small:
        copy.start()
    big = []
    for k in range(CHUNKS):
        part = pl.ds(k * CHUNK, CHUNK)
        second = pl.ds(RUN + k * CHUNK, CHUNK)
        big.append(
            (
                pltpu.make_async_copy(cur_hbm.at[part], cur.at[part], sems.at[0, k]),
                pltpu.make_async_copy(cur_hbm.at[second], cur.at[second], sems.at[1, k]),
                pltpu.make_async_copy(agg_hbm.at[part], maps.at[part], sems.at[2, k]),
            )
        )
    for copies in big[:AHEAD]:
        for copy in copies:
            copy.start()
    for copy in small:
        copy.wait()
    own = [lax.rem(parent[run * RUN], boxes.shape[0]) for run in range(2)]
    coef_copies = [
        pltpu.make_async_copy(coef_hbm.at[own[run]], coef.at[run], small_sems.at[3 + run]) for run in range(2)
    ]
    for copy in coef_copies:
        copy.start()

    def rays(k):
        for copy in big[k]:
            copy.wait()
        for copies in big[k + AHEAD : k + AHEAD + 1]:
            for copy in copies:
                copy.start()
        left = jnp.concatenate([maps[k * CHUNK + i] for i in range(CHUNK)], axis=1)
        right = jnp.concatenate(
            [cur[pl.ds(run * RUN + k * CHUNK, CHUNK)].reshape(CHUNK * UNK, TIME) for run in range(2)], axis=1
        )
        return jnp.dot(left, right, preferred_element_type=F32)

    total[...] = rays(0)
    for k in range(1, CHUNKS // 2):
        total[...] = total[...] + rays(k)
    for copy in coef_copies:
        copy.wait()
    row = lax.broadcasted_iota(jnp.int32, (2 * SLOTS, UNK), 0)
    used = row < jnp.where(row < SLOTS, counts[own[0]], SLOTS + counts[own[1]])
    turned = jnp.where(used, coef[...].reshape(2 * SLOTS, UNK), 0.0).T
    listed = jnp.concatenate([boxes[pl.ds(own[run], 1), :] for run in range(2)], axis=1)
    listed = jnp.broadcast_to(listed.astype(F32), (2 * SLOTS, 2 * SLOTS)).T[:, :1]
    lane = lax.broadcasted_iota(jnp.int32, (2 * SLOTS, 2 * DEVS), 1).astype(F32)
    match = jnp.where(listed == lane, 1.0, 0.0).astype(BF16)
    coef_big, coef_rest = split(turned)
    for run in range(2):
        at = slice(run * SLOTS, (run + 1) * SLOTS)
        weight = jnp.dot(coef_big[:, at], match[at], preferred_element_type=F32) + jnp.dot(
            coef_rest[:, at], match[at], preferred_element_type=F32
        )
        for half in range(2):
            for side in range(2):
                wide[pl.ds(4 + half * 4 + run * 2 + side, DEVS, stride=ROWS), :] = weight[
                    half * DEVS : (half + 1) * DEVS, side * DEVS : (side + 1) * DEVS
                ]
    lane = lax.broadcasted_iota(jnp.int32, (DEVS, TIME), 1)
    wide[pl.ds(12, DEVS, stride=ROWS), :] = jnp.where(lane < RUN, parent[0], parent[RUN]).astype(F32)
    for spare in range(13, ROWS):
        wide[pl.ds(spare, DEVS, stride=ROWS), :] = jnp.zeros((DEVS, TIME), F32)
    for k in range(CHUNKS // 2, CHUNKS):
        total[...] = total[...] + rays(k)
    for half in range(2):
        for run in range(2):
            wide[pl.ds(2 * half + run, DEVS, stride=ROWS), :] = total[
                half * DEVS : (half + 1) * DEVS, run * TIME : (run + 1) * TIME
            ]
    sent[...] = wide[...].astype(BF16)


def around(links, cur, leaf, at):
    def linked(run, side):
        value = cur[run, at + 2 * side - 1]
        return value * links[run * RUN + leaf, side].astype(F32).astype(BF16)

    own = jnp.concatenate([cur[run, at] for run in range(2)], axis=1)
    return [own] + [jnp.concatenate([linked(run, side) for run in range(2)], axis=1) for side in range(2)]


def near(links, cur_hbm, blocks_hbm, out_hbm, cur, blocks, stage, in_sems, blocks_sem, out_sems):
    steps = EARLY // STEP

    def fetch(k, run):
        first = 0 if k == 0 else 2 + k * STEP
        count = 2 + (k + 1) * STEP - first
        return pltpu.make_async_copy(
            cur_hbm.at[pl.ds(run * RUN + EDGE - 1 + first, count)],
            cur.at[run, pl.ds(first, count)],
            in_sems.at[run, k],
        )

    def store(k, run):
        return pltpu.make_async_copy(
            stage.at[run, pl.ds(k * STEP, STEP)], out_hbm.at[run, pl.ds(k * STEP, STEP)], out_sems.at[run, k]
        )

    load = pltpu.make_async_copy(blocks_hbm, blocks, blocks_sem)
    load.start()
    for k in range(steps):
        for run in range(2):
            fetch(k, run).start()
    load.wait()
    left = jnp.concatenate([blocks[j] for j in range(3)], axis=1)
    for k in range(steps):
        for run in range(2):
            fetch(k, run).wait()
        for j in range(k * STEP, (k + 1) * STEP):
            right = jnp.concatenate(around(links, cur, EDGE + j, 1 + j), axis=0)
            done = jnp.dot(left, right, preferred_element_type=F32)
            for run in range(2):
                stage[run, j] = done[:, run * TIME : (run + 1) * TIME].astype(NEAR)
        for run in range(2):
            store(k, run).start()
    for k in range(steps):
        for run in range(2):
            store(k, run).wait()


def translate(got, kernel, out, wide, tall):
    wide[...] = got[...].astype(F32)
    parents = wide[pl.ds(12, DEVS, stride=ROWS), :].T
    source = jnp.concatenate([parents[0:1], parents[RUN : RUN + 1]], axis=1)
    box = lax.broadcasted_iota(jnp.int32, (2 * DEVS, 2 * DEVS), 0).astype(F32)
    place = jnp.where(box == source, 1.0, 0.0).astype(BF16)
    rays = jnp.concatenate(
        [
            jnp.concatenate([wide[pl.ds(2 * half + run, DEVS, stride=ROWS), :] for half in range(2)], axis=1)
            for run in range(2)
        ],
        axis=0,
    )
    rays = jnp.dot(place, rays.astype(BF16), preferred_element_type=F32).astype(BF16)
    lag = jnp.broadcast_to(kernel[...], (TIME, TIME))
    lag = pltpu.roll(lag, 0, 1, stride=1, stride_axis=0)
    row = lax.broadcasted_iota(jnp.int32, (TIME, TIME), 0)
    column = lax.broadcasted_iota(jnp.int32, (TIME, TIME), 1)
    lag_big, lag_rest = split(jnp.where(column >= row, lag, 0.0))
    far = []
    for half in range(2):
        weight = jnp.concatenate(
            [
                jnp.concatenate(
                    [wide[pl.ds(4 + half * 4 + run * 2 + side, DEVS, stride=ROWS), :] for side in range(2)], axis=1
                )
                for run in range(2)
            ],
            axis=0,
        )
        far.append(
            jnp.dot(weight.astype(BF16), rays[:, half * TIME : (half + 1) * TIME], preferred_element_type=F32)
        )
    big, rest = split(jnp.concatenate(far, axis=0))
    done = (
        jnp.dot(big, lag_big, preferred_element_type=F32)
        + jnp.dot(rest, lag_big, preferred_element_type=F32)
        + jnp.dot(big, lag_rest, preferred_element_type=F32)
    )
    for k in range(4):
        tall[pl.ds(k, DEVS, stride=4), :] = done[k * DEVS : (k + 1) * DEVS]
    out[...] = tall[...].astype(BF16)


def disaggregate(
    links, got, low, high, blocks_hbm, cur_hbm, near_hbm, dis_hbm, out_hbm,
    blocks, cur, early, dis, stage, tall, incoming, cur_sems, early_sems, side_sems, out_sems,
):
    late = [(k % 2 * (RUN - EDGE) + k // 2 * STEP) for k in range(2 * EDGE // STEP)]
    early_steps = [EDGE + k * STEP for k in range(EARLY // STEP)]
    order = []
    for k in range(max(len(late), len(early_steps))):
        order += [(k, late[k], True)] if k < len(late) else []
        order += [(k, early_steps[k], False)] if k < len(early_steps) else []

    def fetch(k, first, is_late):
        at = pl.ds(first, STEP)
        copies = [pltpu.make_async_copy(dis_hbm.at[at], dis.at[at], side_sems.at[first // STEP])]
        for run in range(2):
            if is_late:
                start, end = first - 1, first + STEP + 1
                start = max(start, 0) if run == 0 else start
                end = min(end, RUN) if run == 1 else end
                copies.append(
                    pltpu.make_async_copy(
                        cur_hbm.at[pl.ds(run * RUN + start, end - start)],
                        cur.at[k, run, pl.ds(start - first + 1, end - start)],
                        cur_sems.at[run, k],
                    )
                )
            else:
                part = pl.ds(k * STEP, STEP)
                copies.append(
                    pltpu.make_async_copy(near_hbm.at[run, part], early.at[run, part], early_sems.at[run, k])
                )
        return copies

    def store(first, run):
        at = pl.ds(run * RUN + first, STEP)
        return pltpu.make_async_copy(stage.at[at], out_hbm.at[at], out_sems.at[run, first // STEP])

    load = pltpu.make_async_copy(blocks_hbm, blocks, side_sems.at[RUN // STEP])
    load.start()
    for part in order:
        for copy in fetch(*part):
            copy.start()
    cur[late.index(0), 0, 0] = low[...]
    cur[late.index(RUN - STEP), 1, STEP + 1] = high[...]
    tall[...] = got[...].astype(F32)
    for half in range(2):
        for run in range(2):
            incoming[half * DEVS : (half + 1) * DEVS, run * TIME : (run + 1) * TIME] = tall[
                pl.ds(2 * half + run, DEVS, stride=4), :
            ].astype(BF16)
    load.wait()
    left = jnp.concatenate([blocks[j] for j in range(3)], axis=1)
    for part in order:
        for copy in fetch(*part):
            copy.wait()
        k, first, is_late = part
        for j in range(STEP):
            leaf = first + j
            if is_late:
                right = jnp.concatenate(around(links, cur.at[k], leaf, 1 + j) + [incoming[...]], axis=0)
                done = jnp.dot(jnp.concatenate([left, dis[leaf]], axis=1), right, preferred_element_type=F32)
            else:
                done = jnp.dot(dis[leaf], incoming[...], preferred_element_type=F32)
            for run in range(2):
                value = done[:, run * TIME : (run + 1) * TIME]
                if not is_late:
                    value = value + early[run, k * STEP + j].astype(F32)
                stage[run * RUN + leaf] = value.astype(BF16)
        for run in range(2):
            store(first, run).start()
    for part in order:
        for run in range(2):
            store(part[1], run).wait()


def per_device(
    currents,
    leaf_parent,
    near_links,
    near_blocks,
    aggregate_maps,
    far_boxes,
    far_counts,
    translate_coef,
    time_kernel,
    disaggregate_maps,
):
    leaves = 2 * RUN
    hbm = whole(pltpu.HBM)
    first, last = currents[0], currents[leaves - 1]
    sent = pl.pallas_call(
        aggregate,
        out_shape=jax.ShapeDtypeStruct((DEVS * ROWS, TIME), BF16),
        in_specs=[hbm] * 6,
        out_specs=whole(),
        scratch_shapes=[
            pltpu.VMEM((leaves, UNK, TIME), BF16),
            pltpu.VMEM((RUN, UNK, UNK), BF16),
            pltpu.VMEM((2, SLOTS, UNK), F32),
            pltpu.VMEM(far_boxes.shape, jnp.int32),
            pltpu.SMEM(leaf_parent.shape, jnp.int32),
            pltpu.SMEM(far_counts.shape, jnp.int32),
            pltpu.VMEM((DEVS * ROWS, TIME), F32),
            pltpu.VMEM((UNK, UNK), F32),
            pltpu.SemaphoreType.DMA((3, CHUNKS)),
            pltpu.SemaphoreType.DMA((5,)),
        ],
        compiler_params=params(40),
        cost_estimate=pl.CostEstimate(flops=2 << 30, bytes_accessed=17 * MIB, transcendentals=0),
        name="aggregate",
    )(*in_hbm(leaf_parent, far_counts, far_boxes, translate_coef, currents, aggregate_maps))
    arrived = lax.all_to_all(sent.reshape(DEVS, ROWS, TIME), AXES, 0, 0, tiled=True)
    early = pl.pallas_call(
        near,
        out_shape=pltpu.HBM((2, EARLY, UNK, TIME), NEAR),
        in_specs=[whole(pltpu.SMEM)] + [hbm] * 2,
        out_specs=hbm,
        scratch_shapes=[
            pltpu.VMEM((2, EARLY + 2, UNK, TIME), BF16),
            pltpu.VMEM((3, UNK, UNK), BF16),
            pltpu.VMEM((2, EARLY, UNK, TIME), NEAR),
            pltpu.SemaphoreType.DMA((2, EARLY // STEP)),
            pltpu.SemaphoreType.DMA(()),
            pltpu.SemaphoreType.DMA((2, EARLY // STEP)),
        ],
        compiler_params=params(40),
        cost_estimate=pl.CostEstimate(flops=3 << 30, bytes_accessed=12 * MIB, transcendentals=0),
        name="near",
    )(near_links, *in_hbm(currents, near_blocks))
    arrived, early, first, last = lax.optimization_barrier((arrived, early, first, last))
    incoming = pl.pallas_call(
        translate,
        out_shape=jax.ShapeDtypeStruct((DEVS * 4, TIME), BF16),
        in_specs=[whole(), whole()],
        out_specs=whole(),
        scratch_shapes=[pltpu.VMEM((DEVS * ROWS, TIME), F32), pltpu.VMEM((DEVS * 4, TIME), F32)],
        compiler_params=params(12),
        cost_estimate=pl.CostEstimate(flops=1 << 28, bytes_accessed=MIB, transcendentals=0),
        name="translate",
    )(arrived.reshape(DEVS * ROWS, TIME), time_kernel.reshape(1, TIME))
    incoming, first, last = lax.optimization_barrier((incoming, first, last))
    returned = lax.all_to_all(incoming.reshape(DEVS, 4, TIME), AXES, 0, 0, tiled=True)
    low = lax.ppermute(last, AXES, [(i, i + 1) for i in range(DEVS - 1)])
    high = lax.ppermute(first, AXES, [(i + 1, i) for i in range(DEVS - 1)])
    return pl.pallas_call(
        disaggregate,
        out_shape=pltpu.HBM((leaves, UNK, TIME), BF16),
        in_specs=[whole(pltpu.SMEM)] + [whole()] * 3 + [hbm] * 4,
        out_specs=hbm,
        scratch_shapes=[
            pltpu.VMEM((3, UNK, UNK), BF16),
            pltpu.VMEM((2 * EDGE // STEP, 2, STEP + 2, UNK, TIME), BF16),
            pltpu.VMEM((2, EARLY, UNK, TIME), NEAR),
            pltpu.VMEM((RUN, UNK, UNK), BF16),
            pltpu.VMEM((leaves, UNK, TIME), BF16),
            pltpu.VMEM((DEVS * 4, TIME), F32),
            pltpu.VMEM((UNK, UNK), BF16),
            pltpu.SemaphoreType.DMA((2, 2 * EDGE // STEP)),
            pltpu.SemaphoreType.DMA((2, EARLY // STEP)),
            pltpu.SemaphoreType.DMA((RUN // STEP + 1,)),
            pltpu.SemaphoreType.DMA((2, RUN // STEP)),
        ],
        compiler_params=params(50),
        cost_estimate=pl.CostEstimate(flops=5 << 30, bytes_accessed=28 * MIB, transcendentals=0),
        name="disaggregate",
    )(
        near_links,
        returned.reshape(DEVS * 4, TIME),
        low,
        high,
        *in_hbm(near_blocks, currents, early, disaggregate_maps),
    )


def solution(mesh):
    in_specs = (
        P(AXES, None, None),
        P(AXES),
        P(AXES, None),
        P(),
        P(),
        P("box", None),
        P("box"),
        P("box", None, None),
        P(),
        P(),
    )
    return jax.shard_map(
        per_device, mesh=mesh, in_specs=in_specs, out_specs=P(AXES, None, None), check_vma=False
    )
```

time: 116 us -> 66.1 us (0.57)
  the two profiles are of different devices: /device:TPU:1 before, /device:TPU:31 now
where the time goes in v2:
time: 66.1 us; the launch traced here: 65.9 us
  Pallas kernels  31.1 us (47%)
  starting transfers between devices  25.4 us (38%)
  waiting for transfers between devices  8.04 us (12%)
  local copies, waits for them, and re-layouts  1 us (2%)
    pallas_call x1, Pallas kernels, per_device(): pl.pallas_call(disaggregate, out_shape=pltpu.HBM((leaves, UNK, TIME), BF1...  11.8 us
    all_to_all x1, starting transfers between devices, per_device(): lax.all_to_all(sent.reshape(DEVS, ROWS, TIME), AXES, 0, 0, tiled=True)  10.6 us
    all_to_all x1, starting transfers between devices, per_device(): lax.all_to_all(incoming.reshape(DEVS, 4, TIME), AXES, 0, 0, tiled=True)  9.42 us
    pallas_call x1, Pallas kernels, per_device(): pl.pallas_call(aggregate, out_shape=jax.ShapeDtypeStruct((DEVS * ROWS, TI...  8.94 us
    pallas_call x1, Pallas kernels, per_device(): pl.pallas_call(near, out_shape=pltpu.HBM((2, EARLY, UNK, TIME), NEAR), in...  8.88 us
    ppermute x1, waiting for transfers between devices, per_device(): high = lax.ppermute(first, AXES, [(i + 1, i) for i in range(DEVS - 1)])  7.68 us
    ppermute x1, starting transfers between devices, per_device(): low = lax.ppermute(last, AXES, [(i, i + 1) for i in range(DEVS - 1)])  3.35 us
    ppermute x1, starting transfers between devices, per_device(): high = lax.ppermute(first, AXES, [(i + 1, i) for i in range(DEVS - 1)])  2.11 us
  transfers between devices with their start and end apart: 4, of which 2 were waited for; matrix products, arithmetic and copies ran while one was open for 2% of the time, Pallas kernels for 13%

profile of v2, /device:TPU:31, one launch (start us, length us, event | category | flops | bytes accessed | tf_op | source)
XLA Modules:
  0.0 65.9 jit_solution(2264316947207629143)
XLA Ops:
  0.0 0.0 copy-start.1
  0.0 8.9 %aggregate.1 = bf16[2048,128]{1,0:T(8,128)(2,1)} custom-call(s32[128]{0:T(128)} %parent_hbm.1, s32[32]{0:T(128)} %counts_hbm.1, s32[32,64]{1,0:T(8,128)} %boxes_hbm.1, f32[32,64,256]{2,1,0:T(8,128)} %coef_hbm.1, bf16[128,256,128]{2,1,0:T(8,128)(2,1)} %cur_hbm.5, bf16[64,256,256]{2,1,0:T(8,128)(2,1)} %agg_hbm.1), custom_call_target="tpu_custom_call" | custom-call | flops 2147483648 | bytes 17825792 | tf_op jit(solution)/shard_map/aggregate/pallas_call | solution.py:309
  8.9 0.0 copy-start
  9.0 10.6 %all-to-all-start = ((bf16[128,16,128]{2,1,0:T(8,128)(2,1)}), bf16[128,16,128]{2,1,0:T(8,128)(2,1)S(1)}, u32[]{:S(2)}, u32[]{:S(2)}) async-start(bf16[128,16,128]{2,1,0:T(8,128)(2,1)} %bitcast), calls=%async_computation | async-start | bytes 1048576 | tf_op jit(solution)/shard_map/all_to_all | solution.py:330
  19.5 0.0 copy-done.1
  19.5 0.1 copy.12.links
  19.6 0.9 %slice_bitcast_fusion = (bf16[256,128]{1,0:T(8,128)(2,1)S(1)}, bf16[256,128]{1,0:T(8,128)(2,1)S(1)}) fusion(bf16[128,256,128]{2,1,0:T(8,128)(2,1)} %cur_hbm.5), kind=kLoop, calls=%fused_computation | loop fusion | bytes 262144 | tf_op jit(solution)/shard_map/squeeze | solution.py:308
  20.5 8.9 %near.1.near_hbm = bf16[2,32,256,128]{3,2,1,0:T(8,128)(2,1)} custom-call(s32[128,2]{1,0:T(8,128)S(1)} %copy.12.links, bf16[128,256,128]{2,1,0:T(8,128)(2,1)} %cur_hbm.5, bf16[3,256,256]{2,1,0:T(8,128)(2,1)} %blocks_hbm.3), custom_call_target="tpu_custom_call" | custom-call | flops 3221225472 | bytes 12582912 | tf_op jit(solution)/shard_map/near/pallas_call | solution.py:331
  29.4 0.4 all-to-all-done
  29.8 0.0 copy-done
  29.8 1.5 %translate.1 = bf16[512,128]{1,0:T(8,128)(2,1)} custom-call(bf16[2048,128]{1,0:T(8,128)(2,1)S(1)} %bitcast.10, f32[1,128]{1,0:T(1,128)S(1)} %bitcast.11), custom_call_target="tpu_custom_call" | custom-call | flops 268435456 | bytes 1048576 | tf_op jit(solution)/shard_map/translate/pallas_call | solution.py:349
  31.3 9.4 %all-to-all-start.1 = ((bf16[128,4,128]{2,1,0:T(4,128)(2,1)}), bf16[128,4,128]{2,1,0:T(4,128)(2,1)S(1)}, u32[]{:S(2)}, u32[]{:S(2)}) async-start(bf16[128,4,128]{2,1,0:T(4,128)(2,1)} %bitcast.5), calls=%async_computation.1 | async-start | bytes 262144 | tf_op jit(solution)/shard_map/all_to_all | solution.py:360
  40.7 3.4 %collective-permute-start = (bf16[256,128]{1,0:T(8,128)(2,1)S(1)}, bf16[256,128]{1,0:T(8,128)(2,1)S(1)}, u32[]{:S(2)}, u32[]{:S(2)}) collective-permute-start(bf16[256,128]{1,0:T(8,128)(2,1)S(1)} %get-tuple-element.16), channel_id=1, source_target_pairs={{0,1},{1,2},{2,3},{3,4},{4,5},{5,6},{6,7},{7,8},{8,9},{9,10},{10,1... | collective-permute-start | bytes 196616 | tf_op jit(solution)/shard_map/ppermute | solution.py:361
  44.1 2.1 %collective-permute-start.1 = (bf16[256,128]{1,0:T(8,128)(2,1)S(1)}, bf16[256,128]{1,0:T(8,128)(2,1)S(1)}, u32[]{:S(2)}, u32[]{:S(2)}) collective-permute-start(bf16[256,128]{1,0:T(8,128)(2,1)S(1)} %get-tuple-element.17), channel_id=1, source_target_pairs={{1,0},{2,1},{3,2},{4,3},{5,4},{6,5},{7,6},{8,7},{9,8},{10,9},{11,1... | collective-permute-start | bytes 196616 | tf_op jit(solution)/shard_map/ppermute | solution.py:362
  46.2 0.0 collective-permute-done.low
  46.2 7.7 %collective-permute-done.1.high = bf16[256,128]{1,0:T(8,128)(2,1)S(1)} collective-permute-done((bf16[256,128]{1,0:T(8,128)(2,1)S(1)}, bf16[256,128]{1,0:T(8,128)(2,1)S(1)}, u32[]{:S(2)}, u32[]{:S(2)}) %collective-permute-start.1) | collective-permute-done | bytes 65568 | tf_op jit(solution)/shard_map/ppermute | solution.py:362
  53.9 0.0 all-to-all-done.1
  53.9 11.8 %disaggregate.1 = bf16[128,256,128]{2,1,0:T(8,128)(2,1)} custom-call(s32[128,2]{1,0:T(8,128)S(1)} %copy.12.links, bf16[512,128]{1,0:T(8,128)(2,1)S(1)} %bitcast.9, bf16[256,128]{1,0:T(8,128)(2,1)S(1)} %collective-permute-done.low, bf16[256,128]{1,0:T(8,128)(2,1)S(1)} %collective-permute-done.1.high, bf16[3,256,256]{2,1,0:T(8,128)(2,1)} %blocks_hbm.3, ...), custom_call_target="tpu_custom_call" | custom-call | flops 5368709120 | bytes 29360128 | tf_op jit(solution)/shard_map/disaggregate/pallas_call | solution.py:363
Async XLA Ops:
  0.0 19.5 %copy-start.1 = (s32[128,2]{0,1:T(2,128)S(1)}, s32[128,2]{0,1:T(2,128)}, u32[]{:S(2)}) copy-start(s32[128,2]{0,1:T(2,128)} %param.12) | copy-start | bytes 3076
  8.9 20.8 %copy-start = (f32[128]{0:T(128)S(1)}, f32[128]{0:T(128)}, u32[]{:S(2)}) copy-start(f32[128]{0:T(128)} %param.18) | copy-start | bytes 1540
  9.0 20.8 %all-to-all-start = ((bf16[128,16,128]{2,1,0:T(8,128)(2,1)}), bf16[128,16,128]{2,1,0:T(8,128)(2,1)S(1)}, u32[]{:S(2)}, u32[]{:S(2)}) async-start(bf16[128,16,128]{2,1,0:T(8,128)(2,1)} %bitcast), calls=%async_computation | async-start | bytes 1048576 | tf_op jit(solution)/shard_map/all_to_all | solution.py:330
  31.3 22.6 %all-to-all-start.1 = ((bf16[128,4,128]{2,1,0:T(4,128)(2,1)}), bf16[128,4,128]{2,1,0:T(4,128)(2,1)S(1)}, u32[]{:S(2)}, u32[]{:S(2)}) async-start(bf16[128,4,128]{2,1,0:T(4,128)(2,1)} %bitcast.5), calls=%async_computation.1 | async-start | bytes 262144 | tf_op jit(solution)/shard_map/all_to_all | solution.py:360
  40.7 5.5 %collective-permute-start = (bf16[256,128]{1,0:T(8,128)(2,1)S(1)}, bf16[256,128]{1,0:T(8,128)(2,1)S(1)}, u32[]{:S(2)}, u32[]{:S(2)}) collective-permute-start(bf16[256,128]{1,0:T(8,128)(2,1)S(1)} %get-tuple-element.16), channel_id=1, source_target_pairs={{0,1},{1,2},{2,3},{3,4},{4,5},{5,6},{6,7},{7,8},{8,9},{9,10},{10,1... | collective-permute-start | bytes 196616 | tf_op jit(solution)/shard_map/ppermute | solution.py:361
  44.1 9.8 %collective-permute-start.1 = (bf16[256,128]{1,0:T(8,128)(2,1)S(1)}, bf16[256,128]{1,0:T(8,128)(2,1)S(1)}, u32[]{:S(2)}, u32[]{:S(2)}) collective-permute-start(bf16[256,128]{1,0:T(8,128)(2,1)S(1)} %get-tuple-element.17), channel_id=1, source_target_pairs={{1,0},{2,1},{3,2},{4,3},{5,4},{6,5},{7,6},{8,7},{9,8},{10,9},{11,1... | collective-permute-start | bytes 196616 | tf_op jit(solution)/shard_map/ppermute | solution.py:362

commit v3 on v2

--- a/solution.py
+++ b/solution.py
@@ -19,6 +19,8 @@
 DEVS = 128
 ROWS = 16
 F32, BF16 = jnp.float32, jnp.bfloat16
+BACK = 8
+NO_WEIGHT = 2.0**-30
 NEAR = BF16
 MIB = 1 << 20
 
@@ -105,15 +107,13 @@
         weight = jnp.dot(coef_big[:, at], match[at], preferred_element_type=F32) + jnp.dot(
             coef_rest[:, at], match[at], preferred_element_type=F32
         )
+        box = lax.broadcasted_iota(jnp.int32, weight.shape, 1)
+        weight = jnp.where(box == parent[run * RUN], -jnp.maximum(weight, NO_WEIGHT), weight)
         for half in range(2):
             for side in range(2):
                 wide[pl.ds(4 + half * 4 + run * 2 + side, DEVS, stride=ROWS), :] = weight[
                     half * DEVS : (half + 1) * DEVS, side * DEVS : (side + 1) * DEVS
                 ]
-    lane = lax.broadcasted_iota(jnp.int32, (DEVS, TIME), 1)
-    wide[pl.ds(12, DEVS, stride=ROWS), :] = jnp.where(lane < RUN, parent[0], parent[RUN]).astype(F32)
-    for spare in range(13, ROWS):
-        wide[pl.ds(spare, DEVS, stride=ROWS), :] = jnp.zeros((DEVS, TIME), F32)
     for k in range(CHUNKS // 2, CHUNKS):
         total[...] = total[...] + rays(k)
     for half in range(2):
@@ -121,6 +121,11 @@
             wide[pl.ds(2 * half + run, DEVS, stride=ROWS), :] = total[
                 half * DEVS : (half + 1) * DEVS, run * TIME : (run + 1) * TIME
             ]
+    for edge, leaf in enumerate((0, 2 * RUN - 1)):
+        for part in range(2):
+            wide[pl.ds(12 + 2 * edge + part, DEVS, stride=ROWS), :] = cur[
+                leaf, part * DEVS : (part + 1) * DEVS
+            ].astype(F32)
     sent[...] = wide[...].astype(BF16)
 
 
@@ -174,18 +179,14 @@
 
 def translate(got, kernel, out, wide, tall):
     wide[...] = got[...].astype(F32)
-    parents = wide[pl.ds(12, DEVS, stride=ROWS), :].T
-    source = jnp.concatenate([parents[0:1], parents[RUN : RUN + 1]], axis=1)
-    box = lax.broadcasted_iota(jnp.int32, (2 * DEVS, 2 * DEVS), 0).astype(F32)
-    place = jnp.where(box == source, 1.0, 0.0).astype(BF16)
-    rays = jnp.concatenate(
-        [
-            jnp.concatenate([wide[pl.ds(2 * half + run, DEVS, stride=ROWS), :] for half in range(2)], axis=1)
-            for run in range(2)
-        ],
-        axis=0,
-    )
-    rays = jnp.dot(place, rays.astype(BF16), preferred_element_type=F32).astype(BF16)
+    source = lax.broadcasted_iota(jnp.int32, (DEVS, TIME), 0)
+    for part in range(2):
+        first = wide[pl.ds(12 + part, DEVS, stride=ROWS), :]
+        last = wide[pl.ds(14 + part, DEVS, stride=ROWS), :]
+        tall[pl.ds(4 + part, DEVS, stride=BACK), :] = jnp.where(source == 0, 0.0, pltpu.roll(last, 1, 0))
+        tall[pl.ds(6 + part, DEVS, stride=BACK), :] = jnp.where(
+            source == DEVS - 1, 0.0, pltpu.roll(first, DEVS - 1, 0)
+        )
     lag = jnp.broadcast_to(kernel[...], (TIME, TIME))
     lag = pltpu.roll(lag, 0, 1, stride=1, stride_axis=0)
     row = lax.broadcasted_iota(jnp.int32, (TIME, TIME), 0)
@@ -202,9 +203,15 @@
             ],
             axis=0,
         )
-        far.append(
-            jnp.dot(weight.astype(BF16), rays[:, half * TIME : (half + 1) * TIME], preferred_element_type=F32)
-        )
+        if half == 0:
+            place = jnp.where(weight < 0.0, 1.0, 0.0).astype(BF16)
+        weight = jnp.abs(weight)
+        weight = jnp.where(weight > NO_WEIGHT, weight, 0.0).astype(BF16)
+        weight = lax.dot_general(weight, place, (((1,), (1,)), ((), ())), preferred_element_type=F32)
+        rays = jnp.concatenate(
+            [wide[pl.ds(2 * half + run, DEVS, stride=ROWS), :] for run in range(2)], axis=0
+        )
+        far.append(jnp.dot(weight.astype(BF16), rays.astype(BF16), preferred_element_type=F32))
     big, rest = split(jnp.concatenate(far, axis=0))
     done = (
         jnp.dot(big, lag_big, preferred_element_type=F32)
@@ -212,12 +219,12 @@
         + jnp.dot(big, lag_rest, preferred_element_type=F32)
     )
     for k in range(4):
-        tall[pl.ds(k, DEVS, stride=4), :] = done[k * DEVS : (k + 1) * DEVS]
+        tall[pl.ds(k, DEVS, stride=BACK), :] = done[k * DEVS : (k + 1) * DEVS]
     out[...] = tall[...].astype(BF16)
 
 
 def disaggregate(
-    links, got, low, high, blocks_hbm, cur_hbm, near_hbm, dis_hbm, out_hbm,
+    links, got, blocks_hbm, cur_hbm, near_hbm, dis_hbm, out_hbm,
     blocks, cur, early, dis, stage, tall, incoming, cur_sems, early_sems, side_sems, out_sems,
 ):
     late = [(k % 2 * (RUN - EDGE) + k // 2 * STEP) for k in range(2 * EDGE // STEP)]
@@ -258,13 +265,15 @@
     for part in order:
         for copy in fetch(*part):
             copy.start()
-    cur[late.index(0), 0, 0] = low[...]
-    cur[late.index(RUN - STEP), 1, STEP + 1] = high[...]
     tall[...] = got[...].astype(F32)
+    for part in range(2):
+        rows = slice(part * DEVS, (part + 1) * DEVS)
+        cur[late.index(0), 0, 0, rows] = tall[pl.ds(4 + part, DEVS, stride=BACK), :].astype(BF16)
+        cur[late.index(RUN - STEP), 1, STEP + 1, rows] = tall[pl.ds(6 + part, DEVS, stride=BACK), :].astype(BF16)
     for half in range(2):
         for run in range(2):
             incoming[half * DEVS : (half + 1) * DEVS, run * TIME : (run + 1) * TIME] = tall[
-                pl.ds(2 * half + run, DEVS, stride=4), :
+                pl.ds(2 * half + run, DEVS, stride=BACK), :
             ].astype(BF16)
     load.wait()
     left = jnp.concatenate([blocks[j] for j in range(3)], axis=1)
@@ -305,7 +314,6 @@
 ):
     leaves = 2 * RUN
     hbm = whole(pltpu.HBM)
-    first, last = currents[0], currents[leaves - 1]
     sent = pl.pallas_call(
         aggregate,
         out_shape=jax.ShapeDtypeStruct((DEVS * ROWS, TIME), BF16),
@@ -345,25 +353,22 @@
         cost_estimate=pl.CostEstimate(flops=3 << 30, bytes_accessed=12 * MIB, transcendentals=0),
         name="near",
     )(near_links, *in_hbm(currents, near_blocks))
-    arrived, early, first, last = lax.optimization_barrier((arrived, early, first, last))
+    arrived, early = lax.optimization_barrier((arrived, early))
     incoming = pl.pallas_call(
         translate,
-        out_shape=jax.ShapeDtypeStruct((DEVS * 4, TIME), BF16),
+        out_shape=jax.ShapeDtypeStruct((DEVS * BACK, TIME), BF16),
         in_specs=[whole(), whole()],
         out_specs=whole(),
-        scratch_shapes=[pltpu.VMEM((DEVS * ROWS, TIME), F32), pltpu.VMEM((DEVS * 4, TIME), F32)],
+        scratch_shapes=[pltpu.VMEM((DEVS * ROWS, TIME), F32), pltpu.VMEM((DEVS * BACK, TIME), F32)],
         compiler_params=params(12),
         cost_estimate=pl.CostEstimate(flops=1 << 28, bytes_accessed=MIB, transcendentals=0),
         name="translate",
     )(arrived.reshape(DEVS * ROWS, TIME), time_kernel.reshape(1, TIME))
-    incoming, first, last = lax.optimization_barrier((incoming, first, last))
-    returned = lax.all_to_all(incoming.reshape(DEVS, 4, TIME), AXES, 0, 0, tiled=True)
-    low = lax.ppermute(last, AXES, [(i, i + 1) for i in range(DEVS - 1)])
-    high = lax.ppermute(first, AXES, [(i + 1, i) for i in range(DEVS - 1)])
+    returned = lax.all_to_all(incoming.reshape(DEVS, BACK, TIME), AXES, 0, 0, tiled=True)
     return pl.pallas_call(
         disaggregate,
         out_shape=pltpu.HBM((leaves, UNK, TIME), BF16),
-        in_specs=[whole(pltpu.SMEM)] + [whole()] * 3 + [hbm] * 4,
+        in_specs=[whole(pltpu.SMEM)] + [whole()] + [hbm] * 4,
         out_specs=hbm,
         scratch_shapes=[
             pltpu.VMEM((3, UNK, UNK), BF16),
@@ -371,7 +376,7 @@
             pltpu.VMEM((2, EARLY, UNK, TIME), NEAR),
             pltpu.VMEM((RUN, UNK, UNK), BF16),
             pltpu.VMEM((leaves, UNK, TIME), BF16),
-            pltpu.VMEM((DEVS * 4, TIME), F32),
+            pltpu.VMEM((DEVS * BACK, TIME), F32),
             pltpu.VMEM((UNK, UNK), BF16),
             pltpu.SemaphoreType.DMA((2, 2 * EDGE // STEP)),
             pltpu.SemaphoreType.DMA((2, EARLY // STEP)),
@@ -383,9 +388,7 @@
         name="disaggregate",
     )(
         near_links,
-        returned.reshape(DEVS * 4, TIME),
-        low,
-        high,
+        returned.reshape(DEVS * BACK, TIME),
         *in_hbm(near_blocks, currents, early, disaggregate_maps),
     )
 

time: 66.1 us -> 63.2 us (0.956)
  the two profiles are of different devices: /device:TPU:31 before, /device:TPU:1 now
where the time goes in v3:
time: 63.2 us; the launch traced here: 63 us
  Pallas kernels  30.4 us (48%)
  blocking collectives  16.4 us (26%)
  starting transfers between devices  11.5 us (18%)
  waiting for transfers between devices  4.31 us (7%)
    all_to_all x1, blocking collectives, per_device(): lax.all_to_all(incoming.reshape(DEVS, BACK, TIME), AXES, 0, 0, tiled=True)  16.4 us
    pallas_call x1, Pallas kernels, per_device(): pl.pallas_call(disaggregate, out_shape=pltpu.HBM((leaves, UNK, TIME), BF1...  11.8 us
    all_to_all x1, starting transfers between devices, per_device(): lax.all_to_all(sent.reshape(DEVS, ROWS, TIME), AXES, 0, 0, tiled=True)  11.5 us
    pallas_call x1, Pallas kernels, per_device(): pl.pallas_call(near, out_shape=pltpu.HBM((2, EARLY, UNK, TIME), NEAR), in...  8.9 us
    pallas_call x1, Pallas kernels, per_device(): pl.pallas_call(aggregate, out_shape=jax.ShapeDtypeStruct((DEVS * ROWS, TI...  8.85 us
    all_to_all x1, waiting for transfers between devices, per_device(): lax.all_to_all(sent.reshape(DEVS, ROWS, TIME), AXES, 0, 0, tiled=True)  4.31 us
  transfers between devices with their start and end apart: 1, of which 1 were waited for; matrix products, arithmetic and copies ran while one was open for 0% of the time, Pallas kernels for 14%

profile of v3, /device:TPU:1, one launch (start us, length us, event | category | flops | bytes accessed | tf_op | source)
XLA Modules:
  0.0 63.0 jit_solution(5184290050849494327)
XLA Ops:
  0.0 0.0 copy-start.1
  0.0 8.8 %aggregate.1 = bf16[2048,128]{1,0:T(8,128)(2,1)} custom-call(s32[128]{0:T(128)} %parent_hbm.1, s32[32]{0:T(128)} %counts_hbm.1, s32[32,64]{1,0:T(8,128)} %boxes_hbm.1, f32[32,64,256]{2,1,0:T(8,128)} %coef_hbm.1, bf16[128,256,128]{2,1,0:T(8,128)(2,1)} %cur_hbm.5, bf16[64,256,256]{2,1,0:T(8,128)(2,1)} %agg_hbm.1), custom_call_target="tpu_custom_call" | custom-call | flops 2147483648 | bytes 17825792 | tf_op jit(solution)/shard_map/aggregate/pallas_call | solution.py:317
  8.9 0.0 copy-start
  8.9 11.5 %all-to-all-start = ((bf16[128,16,128]{2,1,0:T(8,128)(2,1)}), bf16[128,16,128]{2,1,0:T(8,128)(2,1)S(1)}, u32[]{:S(2)}, u32[]{:S(2)}) async-start(bf16[128,16,128]{2,1,0:T(8,128)(2,1)} %bitcast), calls=%async_computation | async-start | bytes 1048576 | tf_op jit(solution)/shard_map/all_to_all | solution.py:338
  20.4 0.0 copy-done.1
  20.4 0.1 copy.12.links
  20.5 8.9 %near.1.near_hbm = bf16[2,32,256,128]{3,2,1,0:T(8,128)(2,1)} custom-call(s32[128,2]{1,0:T(8,128)S(1)} %copy.12.links, bf16[128,256,128]{2,1,0:T(8,128)(2,1)} %cur_hbm.5, bf16[3,256,256]{2,1,0:T(8,128)(2,1)} %blocks_hbm.3), custom_call_target="tpu_custom_call" | custom-call | flops 3221225472 | bytes 12582912 | tf_op jit(solution)/shard_map/near/pallas_call | solution.py:339
  29.4 4.3 %all-to-all-done = bf16[128,16,128]{2,1,0:T(8,128)(2,1)S(1)} async-done(((bf16[128,16,128]{2,1,0:T(8,128)(2,1)}), bf16[128,16,128]{2,1,0:T(8,128)(2,1)S(1)}, u32[]{:S(2)}, u32[]{:S(2)}) %all-to-all-start) | async-done | bytes 524320 | tf_op jit(solution)/shard_map/all_to_all | solution.py:338
  33.7 0.0 copy-done
  33.7 0.8 %translate.1 = bf16[1024,128]{1,0:T(8,128)(2,1)S(1)} custom-call(bf16[2048,128]{1,0:T(8,128)(2,1)S(1)} %bitcast.6, f32[1,128]{1,0:T(1,128)S(1)} %bitcast.8), custom_call_target="tpu_custom_call" | custom-call | flops 268435456 | bytes 1048576 | tf_op jit(solution)/shard_map/translate/pallas_call | solution.py:357
  34.6 16.4 %all_to_all.10 = bf16[128,8,128]{2,1,0:T(8,128)(2,1)S(1)} all-to-all(bf16[128,8,128]{2,1,0:T(8,128)(2,1)S(1)} %bitcast.7), channel_id=1, replica_groups=mesh['box'=8,'dir'=16] {'box','dir'}, dimensions={0} | all-to-all | bytes 524288 | tf_op jit(solution)/shard_map/all_to_all | solution.py:367
  51.0 11.8 %disaggregate.1 = bf16[128,256,128]{2,1,0:T(8,128)(2,1)} custom-call(s32[128,2]{1,0:T(8,128)S(1)} %copy.12.links, bf16[1024,128]{1,0:T(8,128)(2,1)S(1)} %bitcast.5, bf16[3,256,256]{2,1,0:T(8,128)(2,1)} %blocks_hbm.3, bf16[128,256,128]{2,1,0:T(8,128)(2,1)} %cur_hbm.5, bf16[2,32,256,128]{3,2,1,0:T(8,128)(2,1)} %near.1.near_hbm, bf16[64,256,256]{2,1,0:T(8,128)(2,1)} %dis_hbm.1), custom_call_target="tpu_custom_call" | custom-call | flops 5368709120 | bytes 29360128 | tf_op jit(solution)/shard_map/disaggregate/pallas_call | solution.py:368
Async XLA Ops:
  0.0 20.4 %copy-start.1 = (s32[128,2]{0,1:T(2,128)S(1)}, s32[128,2]{0,1:T(2,128)}, u32[]{:S(2)}) copy-start(s32[128,2]{0,1:T(2,128)} %param.12) | copy-start | bytes 3076
  8.9 24.9 %copy-start = (f32[128]{0:T(128)S(1)}, f32[128]{0:T(128)}, u32[]{:S(2)}) copy-start(f32[128]{0:T(128)} %param.18) | copy-start | bytes 1540
  8.9 24.8 %all-to-all-start = ((bf16[128,16,128]{2,1,0:T(8,128)(2,1)}), bf16[128,16,128]{2,1,0:T(8,128)(2,1)S(1)}, u32[]{:S(2)}, u32[]{:S(2)}) async-start(bf16[128,16,128]{2,1,0:T(8,128)(2,1)} %bitcast), calls=%async_computation | async-start | bytes 1048576 | tf_op jit(solution)/shard_map/all_to_all | solution.py:338

commit v4 on v3

--- a/solution.py
+++ b/solution.py
@@ -14,6 +14,7 @@
 EDGE = (RUN - EARLY) // 2
 STEP = 8
 AHEAD = 3
+KEPT = (0, EDGE)
 UNK = 256
 TIME = 128
 DEVS = 128
@@ -138,7 +139,9 @@
     return [own] + [jnp.concatenate([linked(run, side) for run in range(2)], axis=1) for side in range(2)]
 
 
-def near(links, cur_hbm, blocks_hbm, out_hbm, cur, blocks, stage, in_sems, blocks_sem, out_sems):
+def near(
+    links, cur_hbm, blocks_hbm, dis_hbm, out_hbm, kept, cur, blocks, stage, in_sems, blocks_sem, out_sems, kept_sems
+):
     steps = EARLY // STEP
 
     def fetch(k, run):
@@ -160,6 +163,12 @@
     for k in range(steps):
         for run in range(2):
             fetch(k, run).start()
+    keep = [
+        pltpu.make_async_copy(dis_hbm.at[pl.ds(first, STEP)], kept.at[pl.ds(k * STEP, STEP)], kept_sems.at[k])
+        for k, first in enumerate(KEPT)
+    ]
+    for copy in keep:
+        copy.start()
     load.wait()
     left = jnp.concatenate([blocks[j] for j in range(3)], axis=1)
     for k in range(steps):
@@ -175,6 +184,8 @@
     for k in range(steps):
         for run in range(2):
             store(k, run).wait()
+    for copy in keep:
+        copy.wait()
 
 
 def translate(got, kernel, out, wide, tall):
@@ -224,7 +235,7 @@
 
 
 def disaggregate(
-    links, got, blocks_hbm, cur_hbm, near_hbm, dis_hbm, out_hbm,
+    links, got, kept, blocks_hbm, cur_hbm, near_hbm, dis_hbm, out_hbm,
     blocks, cur, early, dis, stage, tall, incoming, cur_sems, early_sems, side_sems, out_sems,
 ):
     late = [(k % 2 * (RUN - EDGE) + k // 2 * STEP) for k in range(2 * EDGE // STEP)]
@@ -236,7 +247,9 @@
 
     def fetch(k, first, is_late):
         at = pl.ds(first, STEP)
-        copies = [pltpu.make_async_copy(dis_hbm.at[at], dis.at[at], side_sems.at[first // STEP])]
+        copies = []
+        if first not in KEPT:
+            copies.append(pltpu.make_async_copy(dis_hbm.at[at], dis.at[at], side_sems.at[first // STEP]))
         for run in range(2):
             if is_late:
                 start, end = first - 1, first + STEP + 1
@@ -283,11 +296,12 @@
         k, first, is_late = part
         for j in range(STEP):
             leaf = first + j
+            maps = kept[KEPT.index(first) * STEP + j] if first in KEPT else dis[leaf]
             if is_late:
                 right = jnp.concatenate(around(links, cur.at[k], leaf, 1 + j) + [incoming[...]], axis=0)
-                done = jnp.dot(jnp.concatenate([left, dis[leaf]], axis=1), right, preferred_element_type=F32)
+                done = jnp.dot(jnp.concatenate([left, maps], axis=1), right, preferred_element_type=F32)
             else:
-                done = jnp.dot(dis[leaf], incoming[...], preferred_element_type=F32)
+                done = jnp.dot(maps, incoming[...], preferred_element_type=F32)
             for run in range(2):
                 value = done[:, run * TIME : (run + 1) * TIME]
                 if not is_late:
@@ -336,11 +350,14 @@
         name="aggregate",
     )(*in_hbm(leaf_parent, far_counts, far_boxes, translate_coef, currents, aggregate_maps))
     arrived = lax.all_to_all(sent.reshape(DEVS, ROWS, TIME), AXES, 0, 0, tiled=True)
-    early = pl.pallas_call(
+    early, kept = pl.pallas_call(
         near,
-        out_shape=pltpu.HBM((2, EARLY, UNK, TIME), NEAR),
-        in_specs=[whole(pltpu.SMEM)] + [hbm] * 2,
-        out_specs=hbm,
+        out_shape=(
+            pltpu.HBM((2, EARLY, UNK, TIME), NEAR),
+            jax.ShapeDtypeStruct((len(KEPT) * STEP, UNK, UNK), BF16),
+        ),
+        in_specs=[whole(pltpu.SMEM)] + [hbm] * 3,
+        out_specs=(hbm, whole()),
         scratch_shapes=[
             pltpu.VMEM((2, EARLY + 2, UNK, TIME), BF16),
             pltpu.VMEM((3, UNK, UNK), BF16),
@@ -348,12 +365,13 @@
             pltpu.SemaphoreType.DMA((2, EARLY // STEP)),
             pltpu.SemaphoreType.DMA(()),
             pltpu.SemaphoreType.DMA((2, EARLY // STEP)),
+            pltpu.SemaphoreType.DMA((len(KEPT),)),
         ],
         compiler_params=params(40),
         cost_estimate=pl.CostEstimate(flops=3 << 30, bytes_accessed=12 * MIB, transcendentals=0),
         name="near",
-    )(near_links, *in_hbm(currents, near_blocks))
-    arrived, early = lax.optimization_barrier((arrived, early))
+    )(near_links, *in_hbm(currents, near_blocks, disaggregate_maps))
+    arrived, early, kept = lax.optimization_barrier((arrived, early, kept))
     incoming = pl.pallas_call(
         translate,
         out_shape=jax.ShapeDtypeStruct((DEVS * BACK, TIME), BF16),
@@ -368,7 +386,7 @@
     return pl.pallas_call(
         disaggregate,
         out_shape=pltpu.HBM((leaves, UNK, TIME), BF16),
-        in_specs=[whole(pltpu.SMEM)] + [whole()] + [hbm] * 4,
+        in_specs=[whole(pltpu.SMEM)] + [whole()] * 2 + [hbm] * 4,
         out_specs=hbm,
         scratch_shapes=[
             pltpu.VMEM((3, UNK, UNK), BF16),
@@ -389,6 +407,7 @@
     )(
         near_links,
         returned.reshape(DEVS * BACK, TIME),
+        kept,
         *in_hbm(near_blocks, currents, early, disaggregate_maps),
     )
 

time: 63.2 us -> 63 us (level)
  transfers between devices with their start and end apart: 1 -> 1, of which waited for: 1 -> 1; matrix products, arithmetic and copies ran while one was open for 0% -> 0% of each run, Pallas kernels for 14% -> 15%
where the time goes in v4:
time: 63 us; the launch traced here: 62.8 us
  Pallas kernels  30.3 us (48%)
  blocking collectives  16.8 us (27%)
  starting transfers between devices  11.5 us (18%)
  waiting for transfers between devices  3.96 us (6%)
    all_to_all x1, blocking collectives, per_device(): lax.all_to_all(incoming.reshape(DEVS, BACK, TIME), AXES, 0, 0, tiled=True)  16.8 us
    all_to_all x1, starting transfers between devices, per_device(): lax.all_to_all(sent.reshape(DEVS, ROWS, TIME), AXES, 0, 0, tiled=True)  11.5 us
    pallas_call x1, Pallas kernels, per_device(): pl.pallas_call(disaggregate, out_shape=pltpu.HBM((leaves, UNK, TIME), BF1...  11.3 us
    pallas_call x1, Pallas kernels, per_device(): pl.pallas_call(near, out_shape=(pltpu.HBM((2, EARLY, UNK, TIME), NEAR), j...  9.24 us
    pallas_call x1, Pallas kernels, per_device(): pl.pallas_call(aggregate, out_shape=jax.ShapeDtypeStruct((DEVS * ROWS, TI...  8.85 us
    all_to_all x1, waiting for transfers between devices, per_device(): lax.all_to_all(sent.reshape(DEVS, ROWS, TIME), AXES, 0, 0, tiled=True)  3.96 us
  transfers between devices with their start and end apart: 1, of which 1 were waited for; matrix products, arithmetic and copies ran while one was open for 0% of the time, Pallas kernels for 15%

profile of v4, /device:TPU:1, one launch (start us, length us, event | category | flops | bytes accessed | tf_op | source)
XLA Modules:
  0.0 62.8 jit_solution(15784987813975376161)
XLA Ops:
  0.0 0.0 copy-start.1
  0.0 8.8 %aggregate.1 = bf16[2048,128]{1,0:T(8,128)(2,1)} custom-call(s32[128]{0:T(128)} %parent_hbm.1, s32[32]{0:T(128)} %counts_hbm.1, s32[32,64]{1,0:T(8,128)} %boxes_hbm.1, f32[32,64,256]{2,1,0:T(8,128)} %coef_hbm.1, bf16[128,256,128]{2,1,0:T(8,128)(2,1)} %cur_hbm.5, bf16[64,256,256]{2,1,0:T(8,128)(2,1)} %agg_hbm.1), custom_call_target="tpu_custom_call" | custom-call | flops 2147483648 | bytes 17825792 | tf_op jit(solution)/shard_map/aggregate/pallas_call | solution.py:331
  8.9 11.5 %all-to-all-start = ((bf16[128,16,128]{2,1,0:T(8,128)(2,1)}), bf16[128,16,128]{2,1,0:T(8,128)(2,1)S(1)}, u32[]{:S(2)}, u32[]{:S(2)}) async-start(bf16[128,16,128]{2,1,0:T(8,128)(2,1)} %bitcast), calls=%async_computation | async-start | bytes 1048576 | tf_op jit(solution)/shard_map/all_to_all | solution.py:352
  20.4 0.0 copy-done.1
  20.4 0.1 copy.12.links
  20.5 0.0 copy-start
  20.5 9.2 %near.1 = (bf16[2,32,256,128]{3,2,1,0:T(8,128)(2,1)}, bf16[16,256,256]{2,1,0:T(8,128)(2,1)S(1)}) custom-call(s32[128,2]{1,0:T(8,128)S(1)} %copy.12.links, bf16[128,256,128]{2,1,0:T(8,128)(2,1)} %cur_hbm.5, bf16[3,256,256]{2,1,0:T(8,128)(2,1)} %blocks_hbm.3, bf16[64,256,256]{2,1,0:T(8,128)(2,1)} %dis_hbm.3), custom_call_target="tpu_custom_call" | custom-call | flops 3221225472 | bytes 12582912 | tf_op jit(solution)/shard_map/near/pallas_call | solution.py:353
  29.7 4.0 %all-to-all-done = bf16[128,16,128]{2,1,0:T(8,128)(2,1)S(1)} async-done(((bf16[128,16,128]{2,1,0:T(8,128)(2,1)}), bf16[128,16,128]{2,1,0:T(8,128)(2,1)S(1)}, u32[]{:S(2)}, u32[]{:S(2)}) %all-to-all-start) | async-done | bytes 524320 | tf_op jit(solution)/shard_map/all_to_all | solution.py:352
  33.7 0.0 copy-done
  33.7 0.8 %translate.1 = bf16[1024,128]{1,0:T(8,128)(2,1)S(1)} custom-call(bf16[2048,128]{1,0:T(8,128)(2,1)S(1)} %bitcast.6, f32[1,128]{1,0:T(1,128)S(1)} %bitcast.8), custom_call_target="tpu_custom_call" | custom-call | flops 268435456 | bytes 1048576 | tf_op jit(solution)/shard_map/translate/pallas_call | solution.py:375
  34.6 16.8 %all_to_all.10 = bf16[128,8,128]{2,1,0:T(8,128)(2,1)S(1)} all-to-all(bf16[128,8,128]{2,1,0:T(8,128)(2,1)S(1)} %bitcast.7), channel_id=1, replica_groups=mesh['box'=8,'dir'=16] {'box','dir'}, dimensions={0} | all-to-all | bytes 524288 | tf_op jit(solution)/shard_map/all_to_all | solution.py:385
  51.4 11.3 %disaggregate.1 = bf16[128,256,128]{2,1,0:T(8,128)(2,1)} custom-call(s32[128,2]{1,0:T(8,128)S(1)} %copy.12.links, bf16[1024,128]{1,0:T(8,128)(2,1)S(1)} %bitcast.5, bf16[16,256,256]{2,1,0:T(8,128)(2,1)S(1)} %get-tuple-element.13.kept, bf16[3,256,256]{2,1,0:T(8,128)(2,1)} %blocks_hbm.3, bf16[128,256,128]{2,1,0:T(8,128)(2,1)} %cur_hbm.5, ...), custom_call_target="tpu_custom_call" | custom-call | flops 5368709120 | bytes 29360128 | tf_op jit(solution)/shard_map/disaggregate/pallas_call | solution.py:386
Async XLA Ops:
  0.0 20.4 %copy-start.1 = (s32[128,2]{0,1:T(2,128)S(1)}, s32[128,2]{0,1:T(2,128)}, u32[]{:S(2)}) copy-start(s32[128,2]{0,1:T(2,128)} %param.12) | copy-start | bytes 3076
  8.9 24.8 %all-to-all-start = ((bf16[128,16,128]{2,1,0:T(8,128)(2,1)}), bf16[128,16,128]{2,1,0:T(8,128)(2,1)S(1)}, u32[]{:S(2)}, u32[]{:S(2)}) async-start(bf16[128,16,128]{2,1,0:T(8,128)(2,1)} %bitcast), calls=%async_computation | async-start | bytes 1048576 | tf_op jit(solution)/shard_map/all_to_all | solution.py:352
  20.5 13.2 %copy-start = (f32[128]{0:T(128)S(1)}, f32[128]{0:T(128)}, u32[]{:S(2)}) copy-start(f32[128]{0:T(128)} %param.18) | copy-start | bytes 1540

commit v5 on v4

--- a/solution.py
+++ b/solution.py
@@ -14,6 +14,7 @@
 EDGE = (RUN - EARLY) // 2
 STEP = 8
 AHEAD = 3
+WINDOW = 5
 KEPT = (0, EDGE)
 UNK = 256
 TIME = 128
@@ -275,7 +276,7 @@
 
     load = pltpu.make_async_copy(blocks_hbm, blocks, side_sems.at[RUN // STEP])
     load.start()
-    for part in order:
+    for part in order[:WINDOW]:
         for copy in fetch(*part):
             copy.start()
     tall[...] = got[...].astype(F32)
@@ -290,9 +291,12 @@
             ].astype(BF16)
     load.wait()
     left = jnp.concatenate([blocks[j] for j in range(3)], axis=1)
-    for part in order:
+    for n, part in enumerate(order):
         for copy in fetch(*part):
             copy.wait()
+        for ahead in order[n + WINDOW : n + WINDOW + 1]:
+            for copy in fetch(*ahead):
+                copy.start()
         k, first, is_late = part
         for j in range(STEP):
             leaf = first + j

time: 63 us -> 63.1 us (level)
  no operation moved by 1% of the time
where the time goes in v5:
time: 63.1 us; the launch traced here: 62.9 us
  Pallas kernels  30.3 us (48%)
  blocking collectives  16.8 us (27%)
  starting transfers between devices  11.5 us (18%)
  waiting for transfers between devices  3.96 us (6%)
    all_to_all x1, blocking collectives, per_device(): lax.all_to_all(incoming.reshape(DEVS, BACK, TIME), AXES, 0, 0, tiled=True)  16.8 us
    all_to_all x1, starting transfers between devices, per_device(): lax.all_to_all(sent.reshape(DEVS, ROWS, TIME), AXES, 0, 0, tiled=True)  11.5 us
    pallas_call x1, Pallas kernels, per_device(): pl.pallas_call(disaggregate, out_shape=pltpu.HBM((leaves, UNK, TIME), BF1...  11.4 us
    pallas_call x1, Pallas kernels, per_device(): pl.pallas_call(near, out_shape=(pltpu.HBM((2, EARLY, UNK, TIME), NEAR), j...  9.24 us
    pallas_call x1, Pallas kernels, per_device(): pl.pallas_call(aggregate, out_shape=jax.ShapeDtypeStruct((DEVS * ROWS, TI...  8.85 us
    all_to_all x1, waiting for transfers between devices, per_device(): lax.all_to_all(sent.reshape(DEVS, ROWS, TIME), AXES, 0, 0, tiled=True)  3.96 us
  transfers between devices with their start and end apart: 1, of which 1 were waited for; matrix products, arithmetic and copies ran while one was open for 0% of the time, Pallas kernels for 15%

profile of v5, /device:TPU:1, one launch (start us, length us, event | category | flops | bytes accessed | tf_op | source)
XLA Modules:
  0.0 62.9 jit_solution(3602963584105198461)
XLA Ops:
  0.0 0.0 copy-start.1
  0.0 8.8 %aggregate.1 = bf16[2048,128]{1,0:T(8,128)(2,1)} custom-call(s32[128]{0:T(128)} %parent_hbm.1, s32[32]{0:T(128)} %counts_hbm.1, s32[32,64]{1,0:T(8,128)} %boxes_hbm.1, f32[32,64,256]{2,1,0:T(8,128)} %coef_hbm.1, bf16[128,256,128]{2,1,0:T(8,128)(2,1)} %cur_hbm.5, bf16[64,256,256]{2,1,0:T(8,128)(2,1)} %agg_hbm.1), custom_call_target="tpu_custom_call" | custom-call | flops 2147483648 | bytes 17825792 | tf_op jit(solution)/shard_map/aggregate/pallas_call | solution.py:335
  8.9 11.5 %all-to-all-start = ((bf16[128,16,128]{2,1,0:T(8,128)(2,1)}), bf16[128,16,128]{2,1,0:T(8,128)(2,1)S(1)}, u32[]{:S(2)}, u32[]{:S(2)}) async-start(bf16[128,16,128]{2,1,0:T(8,128)(2,1)} %bitcast), calls=%async_computation | async-start | bytes 1048576 | tf_op jit(solution)/shard_map/all_to_all | solution.py:356
  20.4 0.0 copy-done.1
  20.4 0.1 copy.12.links
  20.5 0.0 copy-start
  20.5 9.2 %near.1 = (bf16[2,32,256,128]{3,2,1,0:T(8,128)(2,1)}, bf16[16,256,256]{2,1,0:T(8,128)(2,1)S(1)}) custom-call(s32[128,2]{1,0:T(8,128)S(1)} %copy.12.links, bf16[128,256,128]{2,1,0:T(8,128)(2,1)} %cur_hbm.5, bf16[3,256,256]{2,1,0:T(8,128)(2,1)} %blocks_hbm.3, bf16[64,256,256]{2,1,0:T(8,128)(2,1)} %dis_hbm.3), custom_call_target="tpu_custom_call" | custom-call | flops 3221225472 | bytes 12582912 | tf_op jit(solution)/shard_map/near/pallas_call | solution.py:357
  29.7 4.0 %all-to-all-done = bf16[128,16,128]{2,1,0:T(8,128)(2,1)S(1)} async-done(((bf16[128,16,128]{2,1,0:T(8,128)(2,1)}), bf16[128,16,128]{2,1,0:T(8,128)(2,1)S(1)}, u32[]{:S(2)}, u32[]{:S(2)}) %all-to-all-start) | async-done | bytes 524320 | tf_op jit(solution)/shard_map/all_to_all | solution.py:356
  33.7 0.0 copy-done
  33.7 0.8 %translate.1 = bf16[1024,128]{1,0:T(8,128)(2,1)S(1)} custom-call(bf16[2048,128]{1,0:T(8,128)(2,1)S(1)} %bitcast.6, f32[1,128]{1,0:T(1,128)S(1)} %bitcast.8), custom_call_target="tpu_custom_call" | custom-call | flops 268435456 | bytes 1048576 | tf_op jit(solution)/shard_map/translate/pallas_call | solution.py:379
  34.6 16.8 %all_to_all.10 = bf16[128,8,128]{2,1,0:T(8,128)(2,1)S(1)} all-to-all(bf16[128,8,128]{2,1,0:T(8,128)(2,1)S(1)} %bitcast.7), channel_id=1, replica_groups=mesh['box'=8,'dir'=16] {'box','dir'}, dimensions={0} | all-to-all | bytes 524288 | tf_op jit(solution)/shard_map/all_to_all | solution.py:389
  51.4 11.4 %disaggregate.1 = bf16[128,256,128]{2,1,0:T(8,128)(2,1)} custom-call(s32[128,2]{1,0:T(8,128)S(1)} %copy.12.links, bf16[1024,128]{1,0:T(8,128)(2,1)S(1)} %bitcast.5, bf16[16,256,256]{2,1,0:T(8,128)(2,1)S(1)} %get-tuple-element.13.kept, bf16[3,256,256]{2,1,0:T(8,128)(2,1)} %blocks_hbm.3, bf16[128,256,128]{2,1,0:T(8,128)(2,1)} %cur_hbm.5, ...), custom_call_target="tpu_custom_call" | custom-call | flops 5368709120 | bytes 29360128 | tf_op jit(solution)/shard_map/disaggregate/pallas_call | solution.py:390
Async XLA Ops:
  0.0 20.4 %copy-start.1 = (s32[128,2]{0,1:T(2,128)S(1)}, s32[128,2]{0,1:T(2,128)}, u32[]{:S(2)}) copy-start(s32[128,2]{0,1:T(2,128)} %param.12) | copy-start | bytes 3076
  8.9 24.8 %all-to-all-start = ((bf16[128,16,128]{2,1,0:T(8,128)(2,1)}), bf16[128,16,128]{2,1,0:T(8,128)(2,1)S(1)}, u32[]{:S(2)}, u32[]{:S(2)}) async-start(bf16[128,16,128]{2,1,0:T(8,128)(2,1)} %bitcast), calls=%async_computation | async-start | bytes 1048576 | tf_op jit(solution)/shard_map/all_to_all | solution.py:356
  20.5 13.2 %copy-start = (f32[128]{0:T(128)S(1)}, f32[128]{0:T(128)}, u32[]{:S(2)}) copy-start(f32[128]{0:T(128)} %param.18) | copy-start | bytes 1540
